TPU v7x, 32 devices: a whole 2x2x4 slice. The times are simulated.
32 devices in a mesh: dp: 8 (over z, x), lon: 4 (over y, core).
Axes of the slice: x: 2, y: 2, z: 4, core: 2. Of those that a mesh axis runs over, the one named last changes fastest.
Arguments:
- fields: bfloat16 [8, 32, 48, 768], P('dp', 'lon'), may hold values from -6 to 6
- cotangent: bfloat16 [8, 32, 48, 768], P('dp', 'lon'), may hold values from -6 to 6
- first_weight: bfloat16 [2, 8, 96, 96], replicated, may hold values from -0.4375 to 0.4375
- second_weight: bfloat16 [2, 8, 96, 96], replicated, may hold values from -0.4375 to 0.4375
Outputs:
- layer_out: bfloat16 [8, 32, 48, 768], P('dp', 'lon')
- field_grad: bfloat16 [8, 32, 48, 768], P('dp', 'lon')
- first_grad: float32 [2, 8, 96, 96], replicated
- second_grad: float32 [2, 8, 96, 96], replicated
All inputs are finite; a program needn't handle non-finite values.
Results may differ from a plain program's by a relative error of at most 0.015.
Values may be sent and summed in bfloat16 or wider, within the bound.
No kernel may reach another device: no remote copies, remote signals or barrier semaphores. Data moves between devices by JAX's collectives and lax.ppermute only.
A program may use at most 64 MiB of HBM per device.

v0:
```python
import functools
import math

import jax
import jax.numpy as jnp
import ml_dtypes
import numpy as np
from jax import lax
from jax.experimental import pallas as pl
from jax.experimental.pallas import tpu as pltpu
from jax.sharding import PartitionSpec as P

COEF = 0.7978845608028654
CUBIC = 0.044715


def gelu_value(inner):
    hyper = jnp.tanh(COEF * (inner + CUBIC * inner * inner * inner))
    return 0.5 * inner * (1.0 + hyper)


def gelu_slope(inner):
    hyper = jnp.tanh(COEF * (inner + CUBIC * inner * inner * inner))
    return 0.5 * (1.0 + hyper) + 0.5 * inner * (1.0 - hyper * hyper) * COEF * (
        1.0 + 3.0 * CUBIC * inner * inner
    )


def make_basis(length, count):
    cell_idx = jnp.arange(length, dtype=jnp.int32)
    mode_idx = jnp.arange(count, dtype=jnp.int32)
    product = cell_idx[:, None] * mode_idx[None, :] % length
    angle = product.astype(jnp.float32) * jnp.float32(2.0 * math.pi / length)
    return jnp.stack([jnp.cos(angle), -jnp.sin(angle)], axis=-1).astype(jnp.bfloat16)


def lat_apply(spec, table, lat_scale):
    return (
        jnp.einsum("kphc,phqj->kqjc", spec, table, preferred_element_type=jnp.float32) * lat_scale
    ).astype(jnp.bfloat16)


def forward_weight(weight):
    return jnp.stack([jnp.stack([weight[0], weight[1]]), jnp.stack([-weight[1], weight[0]])])


def adjoint_weight(weight):
    return jnp.stack([jnp.stack([weight[0], -weight[1]]), jnp.stack([weight[1], weight[0]])])


def block_product(spec, stacked):
    return jnp.einsum("kphbi,pqbij->kqhbj", spec, stacked, preferred_element_type=jnp.float32)


def block_adjoint(spec, stacked):
    return jnp.einsum("kphbj,pqbij->kqhbi", spec, stacked, preferred_element_type=jnp.float32)


def block_outer(left, right):
    pairs = jnp.einsum("kphbi,kqhbj->pqbij", left, right, preferred_element_type=jnp.float32)
    return jnp.stack([pairs[0, 0] + pairs[1, 1], pairs[0, 1] - pairs[1, 0]])


def on_device(fields, cotangent, first_weight, second_weight):
    cell_rows = fields[0]
    cot_rows = cotangent[0]
    lat_rows = cell_rows.shape[1]
    channels = cell_rows.shape[2]
    groups = first_weight.shape[1]
    group_width = first_weight.shape[2]
    lon_count = lax.axis_size("lon")
    total_cells = cell_rows.shape[0] * lon_count
    dft_basis = make_basis(total_cells, total_cells // 2)
    lat_basis = make_basis(lat_rows, lat_rows)
    cos_tab = lat_basis[:, :, 0]
    sin_tab = lat_basis[:, :, 1]
    lat_fwd_table = jnp.stack(
        [jnp.stack([cos_tab, sin_tab], axis=1), jnp.stack([-sin_tab, cos_tab], axis=1)], axis=0
    )
    lat_inv_table = jnp.stack(
        [jnp.stack([cos_tab.T, -sin_tab.T], axis=1), jnp.stack([sin_tab.T, cos_tab.T], axis=1)],
        axis=0,
    )
    norm_scale = 1.0 / math.sqrt(total_cells)
    lat_scale = 1.0 / math.sqrt(lat_rows)
    local_modes = cell_rows.shape[0] // 2
    mode_idx = lax.axis_index("lon") * local_modes + jnp.arange(local_modes, dtype=jnp.int32)
    mode_weight = jnp.where(mode_idx == 0, 1.0, 2.0).astype(jnp.bfloat16)[:, None, None, None]
    first_fwd = forward_weight(first_weight)
    second_fwd = forward_weight(second_weight)
    first_adj = adjoint_weight(first_weight)
    second_adj = adjoint_weight(second_weight)

    def local_dft(all_lines):
        return (
            jnp.einsum("whc,wkp->kphc", all_lines, dft_basis, preferred_element_type=jnp.float32)
            * norm_scale
        ).astype(jnp.bfloat16)

    def local_idft(all_modes):
        return (
            jnp.einsum("kphc,wkp->whc", all_modes, dft_basis, preferred_element_type=jnp.float32)
            * norm_scale
        ).astype(jnp.bfloat16)

    def lines_to_modes(all_lines):
        return lax.all_to_all(local_dft(all_lines), "lon", split_axis=0, concat_axis=3, tiled=True)

    def modes_to_lines(all_modes):
        return lax.all_to_all(local_idft(all_modes), "lon", split_axis=0, concat_axis=2, tiled=True)

    def to_spectrum(grid_rows):
        return lines_to_modes(
            lax.all_to_all(grid_rows, "lon", split_axis=2, concat_axis=0, tiled=True)
        )

    def to_cells(spec_rows):
        return modes_to_lines(
            lax.all_to_all(spec_rows, "lon", split_axis=3, concat_axis=0, tiled=True)
        )

    def split_groups(spec_rows):
        return spec_rows.reshape(local_modes, 2, lat_rows, groups, group_width)

    def join_groups(spec_rows):
        return spec_rows.astype(jnp.bfloat16).reshape(local_modes, 2, lat_rows, channels)

    lon_spec = to_spectrum(cell_rows)
    spectrum = split_groups(lat_apply(lon_spec, lat_fwd_table, lat_scale))
    inner = block_product(spectrum, first_fwd)
    act = gelu_value(inner).astype(jnp.bfloat16)
    mixed = join_groups(block_product(act, second_fwd)) * mode_weight
    mixed_lon = lat_apply(mixed, lat_inv_table, lat_scale)
    wave = to_cells(mixed_lon)
    dual_lon = to_spectrum(cot_rows)
    dual = split_groups(lat_apply(dual_lon, lat_fwd_table, lat_scale) * mode_weight)
    back = block_adjoint(dual, second_adj)
    pre = (back * gelu_slope(inner)).astype(jnp.bfloat16)
    back_spec = join_groups(block_adjoint(pre, first_adj))
    back_lon = lat_apply(back_spec, lat_inv_table, lat_scale)
    pull = to_cells(back_lon)
    layer_out = (cell_rows.astype(jnp.float32) + wave.astype(jnp.float32)).astype(jnp.bfloat16)
    field_grad = (cot_rows.astype(jnp.float32) + pull.astype(jnp.float32)).astype(jnp.bfloat16)
    sample_count = lax.axis_size("dp")
    second_term = block_outer(act, dual) / sample_count
    first_term = block_outer(spectrum, pre) / sample_count
    first_grad, second_grad = lax.psum((first_term, second_term), ("dp", "lon"))
    return (layer_out[None], field_grad[None], first_grad, second_grad)


BF = jnp.bfloat16
F32 = jnp.float32


def dft_tables(cells, lat_rows):
    half = cells // 2

    def basis(length, count):
        product = np.arange(length)[:, None] * np.arange(count)[None, :] % length
        angle = product.astype(np.float32) * np.float32(2.0 * math.pi / length)
        pair = np.stack([np.cos(angle), -np.sin(angle)], axis=-1).astype(np.float32)
        return pair.astype(ml_dtypes.bfloat16).astype(np.float64)

    lon = basis(cells, half)[:half]
    lat = basis(lat_rows, lat_rows)
    scale = 1.0 / math.sqrt(cells * lat_rows)
    real = np.einsum("wk,hj->kjwh", lon[..., 0], lat[..., 0]) - np.einsum(
        "wk,hj->kjwh", lon[..., 1], lat[..., 1]
    )
    imag = np.einsum("wk,hj->kjwh", lon[..., 1], lat[..., 0]) + np.einsum(
        "wk,hj->kjwh", lon[..., 0], lat[..., 1]
    )
    both = np.stack([real, imag]) * scale
    size = half * lat_rows
    tables = [both[:, p::2].reshape(size, size).astype(ml_dtypes.bfloat16) for p in (0, 1)]
    forward = np.stack(tables)
    inverse = np.stack([t.T for t in tables])
    return forward, np.ascontiguousarray(inverse)


def dot(left, right):
    return jnp.dot(left, right, preferred_element_type=F32)


def swap_groups(value):
    width = value.shape[-1] // 2
    return jnp.concatenate([value[:, width:], value[:, :width]], axis=1)


def choose(first, second):
    lane = lax.broadcasted_iota(jnp.int32, first.shape, 1)
    return jnp.where(lane < first.shape[1] // 2, first, second)


def pack(rows):
    half = rows.shape[0] // 2
    tail = rows[:, 128:]
    return jnp.concatenate(
        [rows[:, :128], jnp.concatenate([tail[:half], tail[half:]], axis=1)], axis=0
    )


def unpack(packed):
    count = packed.shape[0] * 2 // 3
    tail = packed[count:]
    return jnp.concatenate(
        [packed[:count], jnp.concatenate([tail[:, :64], tail[:, 64:]], axis=0)], axis=1
    )


def pack_kernel(grid_ref, *outs):
    me = lax.axis_index("lon")
    _, cells, lat_rows, channels = grid_ref.shape
    width = channels // 4
    for here in range(4):

        @pl.when(me == here)
        def _():
            rows = grid_ref[...].reshape(cells * lat_rows, channels)
            for slot in range(4):
                there = here ^ slot
                outs[slot][...] = pack(rows[:, there * width : (there + 1) * width])


def weight_kernel(first_ref, second_ref, table_hbm, *refs):
    outs, table_ref, sems = refs[:4], refs[4], refs[5]
    tables = [
        pltpu.make_async_copy(table_hbm.at[p], table_ref.at[p], sems.at[p]) for p in range(2)
    ]
    for copy in tables:
        copy.start()
    for i, weight_ref in enumerate((first_ref, second_ref)):
        for group in range(2):
            real, imag = weight_ref[0, group], weight_ref[1, group]
            cross = imag if group == 0 else -imag
            matrix = jnp.concatenate(
                [
                    jnp.concatenate([real, cross], axis=1),
                    jnp.concatenate([-cross, real], axis=1),
                ],
                axis=0,
            )
            outs[2 * i][group] = matrix
            outs[2 * i + 1][group] = matrix.T
    for copy in tables:
        copy.wait()


def merge_kernel(grid_ref, *refs):
    slots, out_ref = refs[:4], refs[4]
    me = lax.axis_index("lon")
    _, cells, lat_rows, channels = grid_ref.shape
    for here in range(4):

        @pl.when(me == here)
        def _():
            rows = jnp.concatenate([unpack(slots[here ^ s][...]) for s in range(4)], axis=1)
            total = grid_ref[...].astype(F32) + rows.astype(F32).reshape(grid_ref.shape)
            out_ref[...] = total.astype(BF)


def load_halves(me, slots, sums, diffs):
    core = me % 2
    sign = jnp.where(me < 2, 1.0, -1.0).astype(F32)
    for slot, spot in ((0, core), (1, 1 - core)):
        near = slots[slot][...].astype(F32)
        far = slots[slot + 2][...].astype(F32)
        for both, packed in ((sums, near + far), (diffs, sign * (near - far))):
            rows = unpack(packed.astype(BF))
            both[0, spot] = rows
            both[1, spot] = swap_groups(rows)


def to_modes(table, cells):
    size = table.shape[0] // 2
    straight, crossed = (cells[i].reshape(-1, cells.shape[-1]) for i in range(2))
    real = dot(table[:size], straight)
    imag = dot(table[size:], crossed)
    return choose(real, imag), choose(imag, real)


def to_cells(table, first, second):
    return dot(table, jnp.concatenate([choose(first, second), swap_groups(choose(second, first))], axis=0))


def store_halves(me, outs, even, odd, even_ref, odd_ref):
    core = me % 2
    sign = jnp.where(me < 2, 1.0, -1.0).astype(F32)
    even_ref[...] = even.reshape(even_ref.shape)
    odd_ref[...] = odd.reshape(odd_ref.shape)
    for slot, spot in ((0, core), (1, 1 - core)):
        near = even_ref[spot]
        far = sign * odd_ref[spot]
        outs[slot][...] = pack((near + far).astype(BF))
        outs[slot + 2][...] = pack((near - far).astype(BF))


def mode_factor(shape, parity, lat_rows):
    if parity == 1:
        return 2.0
    row = lax.broadcasted_iota(jnp.int32, shape, 0)
    return jnp.where(row < lat_rows, 1.0, 2.0).astype(F32)


def gelu_both(u):
    square = u * u
    hyper = jnp.tanh(COEF * (u + CUBIC * square * u))
    value = 0.5 * u * (1.0 + hyper)
    slope = 0.5 * (1.0 + hyper) + 0.5 * u * (1.0 - hyper * hyper) * COEF * (
        1.0 + 3.0 * CUBIC * square
    )
    return value, slope


def inner_kernel(*refs):
    slots = refs[:4]
    fwd_ref, first_ref = refs[4:6]
    act_ref, slope_ref, spec_t, act_t = refs[6:10]
    sums, diffs = refs[10:]
    load_halves(lax.axis_index("lon"), slots, sums, diffs)
    for parity, half in ((0, sums), (1, diffs)):
        modes = to_modes(fwd_ref[parity], half)
        for group in range(2):
            spec = modes[group].astype(BF)
            act, slope = gelu_both(dot(spec, first_ref[group]))
            act = act.astype(BF)
            size = act.shape[0]
            act_ref[parity, group] = act
            slope_ref[parity, group] = slope
            spec_t[group, :, parity * size : (parity + 1) * size] = spec.T
            act_t[group, :, parity * size : (parity + 1) * size] = act.T


def wave_kernel(lat_rows, act_ref, inv_ref, second_ref, *refs):
    outs = refs[:4]
    even_ref, odd_ref = refs[4:]
    results = []
    for parity in (0, 1):
        factor = mode_factor(act_ref.shape[2:], parity, lat_rows)
        mixed = [
            (dot(act_ref[parity, g], second_ref[g]) * factor).astype(BF) for g in range(2)
        ]
        results.append(to_cells(inv_ref[parity], *mixed))
    store_halves(lax.axis_index("lon"), outs, *results, even_ref, odd_ref)


def weight_terms(full, group):
    size = full.shape[0] // 2
    upper, lower = full[:size], swap_groups(full[size:])
    return choose(upper + lower, upper - lower if group == 0 else lower - upper)


def backward_kernel(lat_rows, *refs):
    slots = refs[:4]
    fwd_ref, second_ref, slope_ref, spec_t, act_t = refs[4:9]
    pre_ref, keep_ref, send_ref = refs[9:12]
    sums, diffs, grad_ref = refs[12:]
    load_halves(lax.axis_index("lon"), slots, sums, diffs)
    terms = [[0.0, 0.0], [0.0, 0.0]]
    for parity, half in ((0, sums), (1, diffs)):
        modes = to_modes(fwd_ref[parity], half)
        factor = mode_factor(modes[0].shape, parity, lat_rows)
        size = modes[0].shape[0]
        span = slice(parity * size, (parity + 1) * size)
        for group in range(2):
            dual = (modes[group] * factor).astype(BF)
            pre = (dot(dual, second_ref[group]) * slope_ref[parity, group]).astype(BF)
            pre_ref[parity, group] = pre
            terms[0][group] += dot(spec_t[group, :, span], pre)
            terms[1][group] += dot(act_t[group, :, span], dual)
    whole = jnp.concatenate([weight_terms(terms[t][g], g) for t in range(2) for g in range(2)], axis=0)
    grad_ref[...] = pack(whole.astype(BF)).reshape(grad_ref.shape)
    side = lax.axis_index("dp") % 2
    keep_ref[...] = grad_ref[side]
    send_ref[...] = grad_ref[1 - side]


def return_kernel(pre_ref, inv_ref, first_ref, *refs):
    outs = refs[:4]
    even_ref, odd_ref = refs[4:]
    results = []
    for parity in (0, 1):
        spec = [dot(pre_ref[parity, g], first_ref[g]).astype(BF) for g in range(2)]
        results.append(to_cells(inv_ref[parity], *spec))
    store_halves(lax.axis_index("lon"), outs, *results, even_ref, odd_ref)


def spread_kernel(scale, *refs):
    pieces, outs, whole, held, sems = refs[:8], refs[8:10], refs[10], refs[11], refs[12]
    me, side = lax.axis_index("lon"), lax.axis_index("dp") % 2
    width = held.shape[-1]
    copies = []
    for slot in (0, 1, 2, 3):
        source = me ^ slot
        whole[side] = pieces[2 * slot][...]
        whole[1 - side] = pieces[2 * slot + 1][...]
        rows = unpack(whole[...].reshape(-1, whole.shape[-1])).astype(F32) * scale
        for tensor in range(2):
            for group in range(2):
                start = (tensor * 2 + group) * width
                block = rows[start : start + width]
                held[slot, tensor, 0, group] = block[:, :width]
                held[slot, tensor, 1, group] = block[:, width:]
            copy = pltpu.make_async_copy(
                held.at[slot, tensor],
                outs[tensor].at[:, pl.ds(2 * source, 2)],
                sems.at[slot, tensor],
            )
            copy.start()
            copies.append(copy)
    for copy in copies:
        copy.wait()


VMEM = pl.BlockSpec(memory_space=pltpu.VMEM)
HBM = pl.BlockSpec(memory_space=pltpu.HBM)


def call(kernel, outs, args, scratch=(), in_hbm=(), out_hbm=False, vmem_mib=20):
    return pl.pallas_call(
        kernel,
        out_shape=outs,
        in_specs=[HBM if i in in_hbm else VMEM for i in range(len(args))],
        out_specs=[HBM if out_hbm else VMEM] * len(outs),
        scratch_shapes=scratch,
        compiler_params=pltpu.CompilerParams(vmem_limit_bytes=vmem_mib * 2**20),
        cost_estimate=pl.CostEstimate(flops=1, bytes_accessed=1, transcendentals=0),
    )(*args)


def swap(value, axis, mask):
    size = lax.axis_size(axis)
    return lax.ppermute(value, axis, [(i, i ^ mask) for i in range(size)])


def flip_pairs(dp_count, lon_count, dp_mask, lon_mask):
    return [
        (d * lon_count + i, (d ^ dp_mask) * lon_count + (i ^ lon_mask))
        for d in range(dp_count)
        for i in range(lon_count)
    ]


def after(*values):
    return lax.optimization_barrier(values)


def added(left, right):
    return (left.astype(F32) + right.astype(F32)).astype(BF)


def by_groups(fields, cotangent, first_weight, second_weight):
    _, cells, lat_rows, channels = fields.shape
    groups, group_width = first_weight.shape[1], first_weight.shape[2]
    lon_count = lax.axis_size("lon")
    sample_count = lax.axis_size("dp")
    width = groups // lon_count * group_width
    total_cells = cells * lon_count
    rows = cells * lat_rows
    half = 2 * rows
    forward, inverse = (jnp.asarray(t) for t in dft_tables(total_cells, lat_rows))
    packed = jax.ShapeDtypeStruct((rows * width // 128, 128), BF)
    piece = jax.ShapeDtypeStruct((4 * group_width * width // 256, 128), BF)

    def trade(slots):
        across, corner, beside = (swap(slots[m], "lon", m) for m in (2, 3, 1))
        return [slots[0], beside, across, corner]

    def own(weight):
        return lax.dynamic_slice_in_dim(weight, lax.axis_index("lon") * 2, 2, axis=1)

    halves = [pltpu.VMEM((2, 2, rows, width), BF)] * 2
    results = [pltpu.VMEM((2, rows, width), F32)] * 2

    field_slots = trade(call(pack_kernel, [packed] * 4, [fields]))
    cot_slots = trade(call(pack_kernel, [packed] * 4, [cotangent]))
    matrix = jax.ShapeDtypeStruct((2, width, width), BF)
    table = jax.ShapeDtypeStruct(forward.shape, BF)
    first_mat, first_adj, second_mat, second_adj, forward = call(
        weight_kernel,
        [matrix] * 4 + [table],
        [own(first_weight), own(second_weight), forward],
        [pltpu.SemaphoreType.DMA((2,))],
        in_hbm=(2,),
        vmem_mib=48,
    )
    modes_shape = jax.ShapeDtypeStruct((2, 2, rows, width), BF)
    slope_shape = jax.ShapeDtypeStruct((2, 2, rows, width), F32)
    turned_shape = jax.ShapeDtypeStruct((2, width, half), BF)
    act, slope, spec_t, act_t = call(
        inner_kernel,
        [modes_shape, slope_shape, turned_shape, turned_shape],
        [*field_slots, forward, first_mat],
        halves,
    )
    wave = call(
        functools.partial(wave_kernel, lat_rows), [packed] * 4, [act, inverse, second_mat], results
    )
    wave_slots = trade(wave)
    cot_slots, wave = after(cot_slots, wave)
    pre, keep, send = call(
        functools.partial(backward_kernel, lat_rows),
        [modes_shape, piece, piece],
        [*cot_slots, forward, second_adj, slope, spec_t, act_t],
        halves + [pltpu.VMEM((2, *piece.shape), BF)],
    )
    other = swap(send, "dp", 1)
    pull = call(return_kernel, [packed] * 4, [pre, inverse, first_adj], results)
    other, pull, wave_slots = after(other, pull, wave_slots)
    pull_slots = trade(pull)
    grad = added(keep, other)
    grid_shape = jax.ShapeDtypeStruct(fields.shape, BF)
    (layer_out,) = call(merge_kernel, [grid_shape], [fields, *wave_slots])
    mask = 2
    while mask < sample_count:
        other = swap(grad, "dp", mask)
        if mask == 4:
            other, layer_out, pull_slots = after(other, layer_out, pull_slots)
        grad = added(grad, other)
        mask *= 2
    beside = swap(grad, "lon", 1)
    beside, pull_slots = after(beside, pull_slots)
    (field_grad,) = call(merge_kernel, [grid_shape], [cotangent, *pull_slots])
    pieces = []
    for lon_mask in (0, 2):
        for dp_mask in (0, 1):
            pairs = flip_pairs(sample_count, lon_count, dp_mask, lon_mask)
            pieces.append(lax.ppermute(grad, ("dp", "lon"), pairs) if dp_mask + lon_mask else grad)
    pieces[3], field_grad = after(pieces[3], field_grad)
    across = [beside] + [swap(p, "lon", 1) for p in pieces[1:]]
    ordered = pieces[:2] + across[:2] + pieces[2:] + across[2:]
    grad_shape = jax.ShapeDtypeStruct(first_weight.shape, F32)
    first_grad, second_grad = call(
        functools.partial(spread_kernel, 1.0 / sample_count),
        [grad_shape] * 2,
        ordered,
        [
            pltpu.VMEM((2, *piece.shape), BF),
            pltpu.VMEM((4, 2, 2, 2, group_width, group_width), F32),
            pltpu.SemaphoreType.DMA((4, 2)),
        ],
        out_hbm=True,
    )
    return layer_out, field_grad, first_grad, second_grad


def owns_groups(mesh, fields, first_weight):
    lon_count, sample_count = mesh.shape["lon"], mesh.shape["dp"]
    _, cells, lat_rows, _ = fields.shape
    return (
        lon_count == 4
        and sample_count > 1
        and sample_count & (sample_count - 1) == 0
        and fields.shape[0] == sample_count
        and first_weight.shape[1:] == (8, 96, 96)
        and lat_rows % 16 == 0
        and cells % 8 == 0
    )


def solution(mesh):
    placed = (P("dp", "lon", None, None), P("dp", "lon", None, None), P(), P())

    def run(fields, cotangent, first_weight, second_weight):
        body = by_groups if owns_groups(mesh, fields, first_weight) else on_device
        return jax.shard_map(
            body, mesh=mesh, in_specs=placed, out_specs=placed, check_vma=False
        )(fields, cotangent, first_weight, second_weight)

    return run
```

profile of v0, /device:TPU:0, one launch (start us, length us, event | category | flops | bytes accessed | tf_op | source)
XLA Modules:
  0.0 46.4 jit_solution(16787830143778317293)
XLA Ops:
  0.6 1.1 %copy-done.1 = bf16[1,8,48,768]{3,2,1,0:T(8,128)(2,1)S(1)} copy-done((bf16[1,8,48,768]{3,2,1,0:T(8,128)(2,1)S(1)}, bf16[1,8,48,768]{3,2,1,0:T(8,128)(2,1)}, u32[]{:S(2)}) %copy-start.1) | copy-done | bytes 589848
  2.5 2.6 %collective-permute-start.4 = (bf16[576,128]{1,0:T(8,128)(2,1)S(1)}, bf16[576,128]{1,0:T(8,128)(2,1)S(1)}, u32[]{:S(2)}, u32[]{:S(2)}) collective-permute-start(bf16[576,128]{1,0:T(8,128)(2,1)S(1)} %get-tuple-element.66), channel_id=1, source_target_pairs={{0,2},{1,3},{2,0},{3,1},{4,6},{5,7},{6,4},{7,5},{8,10},{9,11},{10,... | collective-permute-start | bytes 442376 | tf_op jit(solution)/shard_map/ppermute | solution.py:433
  5.2 1.1 %copy-done.3 = bf16[1,8,48,768]{3,2,1,0:T(8,128)(2,1)S(1)} copy-done((bf16[1,8,48,768]{3,2,1,0:T(8,128)(2,1)S(1)}, bf16[1,8,48,768]{3,2,1,0:T(8,128)(2,1)}, u32[]{:S(2)}) %copy-start.3) | copy-done | bytes 589848
  6.7 1.9 %collective-permute-start.1 = (bf16[576,128]{1,0:T(8,128)(2,1)S(1)}, bf16[576,128]{1,0:T(8,128)(2,1)S(1)}, u32[]{:S(2)}, u32[]{:S(2)}) collective-permute-start(bf16[576,128]{1,0:T(8,128)(2,1)S(1)} %get-tuple-element.62), channel_id=1, source_target_pairs={{0,2},{1,3},{2,0},{3,1},{4,6},{5,7},{6,4},{7,5},{8,10},{9,11},{10,... | collective-permute-start | bytes 442376 | tf_op jit(solution)/shard_map/ppermute | solution.py:433
  8.6 1.0 %constant_dynamic-slice_fusion = (bf16[2,2,96,96]{3,2,1,0:T(8,128)(2,1)S(1)}, bf16[2,2,96,96]{3,2,1,0:T(8,128)(2,1)S(1)}) fusion(bf16[2,8,96,96]{3,2,1,0:T(8,128)(2,1)} %param.9, s32[]{:T(128)S(6)} %select_n.4, bf16[2,8,96,96]{3,2,1,0:T(8,128)(2,1)} %param.8), kind=kLoop, calls=%fused_computation.3 | loop fusion | bytes 294916 | tf_op jit(solution)/shard_map/dynamic_slice | solution.py:470
  9.6 1.7 %copy-done.5 = bf16[2,768,768]{2,1,0:T(8,128)(2,1)S(1)} copy-done((bf16[2,768,768]{2,1,0:T(8,128)(2,1)S(1)}, bf16[2,768,768]{2,1,0:T(8,128)(2,1)}, u32[]{:S(2)}) %copy-start.5) | copy-done | bytes 2359320
  11.3 0.8 %shard_map.95 = (bf16[2,192,192]{2,1,0:T(8,128)(2,1)S(1)}, bf16[2,192,192]{2,1,0:T(8,128)(2,1)S(1)}, bf16[2,192,192]{2,1,0:T(8,128)(2,1)S(1)}, bf16[2,192,192]{2,1,0:T(8,128)(2,1)S(1)}, bf16[2,768,768]{2,1,0:T(8,128)(2,1)S(1)}) custom-call(bf16[2,2,96,96]{3,2,1,0:T(8,128)(2,1)S(1)} %get-tuple-element.117.first_ref, ...), custom_call_target="tpu_custom_call" | custom-call | flops 1 | bytes 1 | tf_op jit(solution)/shard_map/pallas_call | solution.py:420
  12.4 2.2 %shard_map.96 = (bf16[2,2,384,192]{3,2,1,0:T(8,128)(2,1)S(1)}, f32[2,2,384,192]{3,2,1,0:T(8,128)S(1)}, bf16[2,192,768]{2,1,0:T(8,128)(2,1)S(1)}, bf16[2,192,768]{2,1,0:T(8,128)(2,1)S(1)}) custom-call(bf16[576,128]{1,0:T(8,128)(2,1)S(1)} %get-tuple-element.64.refs_0_, bf16[576,128]{1,0:T(8,128)(2,1)S(1)} %collective-permute-done.3.refs_1_, ...), custom_call_target="tpu_custom_call" | custom-call | flops 1 | bytes 1 | tf_op jit(solution)/shard_map/pallas_call | solution.py:420
  14.6 1.4 %shard_map.97 = (bf16[576,128]{1,0:T(8,128)(2,1)S(1)}, bf16[576,128]{1,0:T(8,128)(2,1)S(1)}, bf16[576,128]{1,0:T(8,128)(2,1)S(1)}, bf16[576,128]{1,0:T(8,128)(2,1)S(1)}) custom-call(bf16[2,2,384,192]{3,2,1,0:T(8,128)(2,1)S(1)} %get-tuple-element.70.act_ref, bf16[2,768,768]{2,1,0:T(8,128)(2,1)S(1)} %copy-done, ...), custom_call_target="tpu_custom_call" | custom-call | flops 1 | bytes 1 | tf_op jit(solution)/shard_map/pallas_call | solution.py:420
  16.4 1.9 %collective-permute-start.8 = (bf16[576,128]{1,0:T(8,128)(2,1)S(1)}, bf16[576,128]{1,0:T(8,128)(2,1)S(1)}, u32[]{:S(2)}, u32[]{:S(2)}) collective-permute-start(bf16[576,128]{1,0:T(8,128)(2,1)S(1)} %get-tuple-element.74), channel_id=1, source_target_pairs={{0,2},{1,3},{2,0},{3,1},{4,6},{5,7},{6,4},{7,5},{8,10},{9,11},{10,... | collective-permute-start | bytes 442376 | tf_op jit(solution)/shard_map/ppermute | solution.py:433
  18.7 2.1 %shard_map.98 = (bf16[2,2,384,192]{3,2,1,0:T(8,128)(2,1)S(1)}, bf16[288,128]{1,0:T(8,128)(2,1)S(1)}, bf16[288,128]{1,0:T(8,128)(2,1)S(1)}) custom-call(bf16[576,128]{1,0:T(8,128)(2,1)S(1)} %get-tuple-element.76.refs_0_, bf16[576,128]{1,0:T(8,128)(2,1)S(1)} %collective-permute-done.refs_1_, bf16[576,128]{1,0:T(8,128)(2,1)S(1)} %collective-permute-done.1.refs_2_, ...), custom_call_target="tpu_custom_call" | custom-call | flops 1 | bytes 1 | tf_op jit(solution)/shard_map/pallas_call | solution.py:420
  20.9 1.6 %collective-permute-start.6 = (bf16[288,128]{1,0:T(8,128)(2,1)S(1)}, bf16[288,128]{1,0:T(8,128)(2,1)S(1)}, u32[]{:S(2)}, u32[]{:S(2)}) collective-permute-start(bf16[288,128]{1,0:T(8,128)(2,1)S(1)} %get-tuple-element.85), channel_id=1, source_target_pairs={{0,4},{4,0},{8,12},{12,8},{16,20},{20,16},{24,28},{28,24},{1,5},{5... | collective-permute-start | bytes 221192 | tf_op jit(solution)/shard_map/ppermute | solution.py:433
  22.5 1.3 %shard_map.99 = (bf16[576,128]{1,0:T(8,128)(2,1)S(1)}, bf16[576,128]{1,0:T(8,128)(2,1)S(1)}, bf16[576,128]{1,0:T(8,128)(2,1)S(1)}, bf16[576,128]{1,0:T(8,128)(2,1)S(1)}) custom-call(bf16[2,2,384,192]{3,2,1,0:T(8,128)(2,1)S(1)} %get-tuple-element.86.pre_ref, bf16[2,768,768]{2,1,0:T(8,128)(2,1)S(1)} %copy-done, ...), custom_call_target="tpu_custom_call" | custom-call | flops 1 | bytes 1 | tf_op jit(solution)/shard_map/pallas_call | solution.py:420
  23.8 1.5 %collective-permute-done.6 = bf16[288,128]{1,0:T(8,128)(2,1)S(1)} collective-permute-done((bf16[288,128]{1,0:T(8,128)(2,1)S(1)}, bf16[288,128]{1,0:T(8,128)(2,1)S(1)}, u32[]{:S(2)}, u32[]{:S(2)}) %collective-permute-start.6) | collective-permute-done | bytes 73760 | tf_op jit(solution)/shard_map/ppermute | solution.py:433
  25.3 1.8 %collective-permute-start.10 = (bf16[288,128]{1,0:T(8,128)(2,1)S(1)}, bf16[288,128]{1,0:T(8,128)(2,1)S(1)}, u32[]{:S(2)}, u32[]{:S(2)}) collective-permute-start(bf16[288,128]{1,0:T(8,128)(2,1)S(1)} %add_convert_fusion.2), channel_id=1, source_target_pairs={{0,8},{4,12},{8,0},{12,4},{16,24},{20,28},{24,16},{28,20},{1,9},{5... | collective-permute-start | bytes 221192 | tf_op jit(solution)/shard_map/ppermute | solution.py:433
  27.2 1.5 %collective-permute-start.13 = (bf16[576,128]{1,0:T(8,128)(2,1)S(1)}, bf16[576,128]{1,0:T(8,128)(2,1)S(1)}, u32[]{:S(2)}, u32[]{:S(2)}) collective-permute-start(bf16[576,128]{1,0:T(8,128)(2,1)S(1)} %get-tuple-element.99), channel_id=1, source_target_pairs={{0,2},{1,3},{2,0},{3,1},{4,6},{5,7},{6,4},{7,5},{8,10},{9,11},{10,... | collective-permute-start | bytes 442376 | tf_op jit(solution)/shard_map/ppermute | solution.py:433
  29.8 2.8 %collective-permute-start.11 = (bf16[288,128]{1,0:T(8,128)(2,1)S(1)}, bf16[288,128]{1,0:T(8,128)(2,1)S(1)}, u32[]{:S(2)}, u32[]{:S(2)}) collective-permute-start(bf16[288,128]{1,0:T(8,128)(2,1)S(1)} %add_convert_fusion.1), channel_id=1, source_target_pairs={{0,16},{4,20},{8,24},{12,28},{16,0},{20,4},{24,8},{28,12},{1,17},{... | collective-permute-start | bytes 221192 | tf_op jit(solution)/shard_map/ppermute | solution.py:433
  32.6 1.1 %shard_map.100 = bf16[1,8,48,768]{3,2,1,0:T(8,128)(2,1)} custom-call(bf16[1,8,48,768]{3,2,1,0:T(8,128)(2,1)S(1)} %copy-done.2, bf16[576,128]{1,0:T(8,128)(2,1)S(1)} %get-tuple-element.93.refs_0_, bf16[576,128]{1,0:T(8,128)(2,1)S(1)} %collective-permute-done.7.refs_1_, bf16[576,128]{1,0:T(8,128)(2,1)S(1)} %collective-permute-done.8.refs_2_, ...), custom_call_target="tpu_custom_call" | custom-call | flops 1 | bytes 1 | tf_op jit(solution)/shard_map/pallas_call | solution.py:420
  33.7 1.8 %collective-permute-done.11 = bf16[288,128]{1,0:T(8,128)(2,1)S(1)} collective-permute-done((bf16[288,128]{1,0:T(8,128)(2,1)S(1)}, bf16[288,128]{1,0:T(8,128)(2,1)S(1)}, u32[]{:S(2)}, u32[]{:S(2)}) %collective-permute-start.11) | collective-permute-done | bytes 73760 | tf_op jit(solution)/shard_map/ppermute | solution.py:433
  36.5 2.4 %collective-permute-start.15 = (bf16[288,128]{1,0:T(8,128)(2,1)S(1)}, bf16[288,128]{1,0:T(8,128)(2,1)S(1)}, u32[]{:S(2)}, u32[]{:S(2)}) collective-permute-start(bf16[288,128]{1,0:T(8,128)(2,1)S(1)} %add_convert_fusion.refs_0_), channel_id=1, source_target_pairs={{0,6},{1,7},{2,4},{3,5},{4,2},{5,3},{6,0},{7,1},{8,14},{9,15},{10,... | collective-permute-start | bytes 221192 | tf_op jit(solution)/shard_map/ppermute | solution.py:528
  40.0 1.1 %shard_map.101 = bf16[1,8,48,768]{3,2,1,0:T(8,128)(2,1)} custom-call(bf16[1,8,48,768]{3,2,1,0:T(8,128)(2,1)S(1)} %copy-done.4, bf16[576,128]{1,0:T(8,128)(2,1)S(1)} %get-tuple-element.107.refs_0_, bf16[576,128]{1,0:T(8,128)(2,1)S(1)} %collective-permute-done.12.refs_1_, bf16[576,128]{1,0:T(8,128)(2,1)S(1)} %collective-permute-done.13.refs_2_, ...), custom_call_target="tpu_custom_call" | custom-call | flops 1 | bytes 1 | tf_op jit(solution)/shard_map/pallas_call | solution.py:420
  41.0 1.3 %collective-permute-done.15.refs_5_ = bf16[288,128]{1,0:T(8,128)(2,1)S(1)} collective-permute-done((bf16[288,128]{1,0:T(8,128)(2,1)S(1)}, bf16[288,128]{1,0:T(8,128)(2,1)S(1)}, u32[]{:S(2)}, u32[]{:S(2)}) %collective-permute-start.15) | collective-permute-done | bytes 73760 | tf_op jit(solution)/shard_map/ppermute | solution.py:528
  42.3 1.2 %collective-permute-done.17.refs_1_ = bf16[288,128]{1,0:T(8,128)(2,1)S(1)} collective-permute-done((bf16[288,128]{1,0:T(8,128)(2,1)S(1)}, bf16[288,128]{1,0:T(8,128)(2,1)S(1)}, u32[]{:S(2)}, u32[]{:S(2)}) %collective-permute-start.17) | collective-permute-done | bytes 73760 | tf_op jit(solution)/shard_map/ppermute | solution.py:528
  45.1 1.4 %shard_map.102 = (f32[2,8,96,96]{3,2,1,0:T(8,128)}, f32[2,8,96,96]{3,2,1,0:T(8,128)}) custom-call(bf16[288,128]{1,0:T(8,128)(2,1)S(1)} %add_convert_fusion.refs_0_, bf16[288,128]{1,0:T(8,128)(2,1)S(1)} %collective-permute-done.17.refs_1_, bf16[288,128]{1,0:T(8,128)(2,1)S(1)} %collective-permute-done.16.refs_2_, ...), custom_call_target="tpu_custom_call" | custom-call | flops 1 | bytes 1 | tf_op jit(solution)/shard_map/pallas_call | solution.py:420
  (46 shorter events, 7.4 us)
Async XLA Ops:
  2.0 6.6 %collective-permute-start.3 = (bf16[576,128]{1,0:T(8,128)(2,1)S(1)}, bf16[576,128]{1,0:T(8,128)(2,1)S(1)}, u32[]{:S(2)}, u32[]{:S(2)}) collective-permute-start(bf16[576,128]{1,0:T(8,128)(2,1)S(1)} %get-tuple-element.65), channel_id=1, source_target_pairs={{0,1},{1,0},{2,3},{3,2},{4,5},{5,4},{6,7},{7,6},{8,9},{9,8},{10,11... | collective-permute-start | bytes 442376 | tf_op jit(solution)/shard_map/ppermute | solution.py:433
  2.5 9.5 %collective-permute-start.4 = (bf16[576,128]{1,0:T(8,128)(2,1)S(1)}, bf16[576,128]{1,0:T(8,128)(2,1)S(1)}, u32[]{:S(2)}, u32[]{:S(2)}) collective-permute-start(bf16[576,128]{1,0:T(8,128)(2,1)S(1)} %get-tuple-element.66), channel_id=1, source_target_pairs={{0,2},{1,3},{2,0},{3,1},{4,6},{5,7},{6,4},{7,5},{8,10},{9,11},{10,... | collective-permute-start | bytes 442376 | tf_op jit(solution)/shard_map/ppermute | solution.py:433
  5.1 7.3 %collective-permute-start.5 = (bf16[576,128]{1,0:T(8,128)(2,1)S(1)}, bf16[576,128]{1,0:T(8,128)(2,1)S(1)}, u32[]{:S(2)}, u32[]{:S(2)}) collective-permute-start(bf16[576,128]{1,0:T(8,128)(2,1)S(1)} %get-tuple-element.67), channel_id=1, source_target_pairs={{0,3},{1,2},{2,1},{3,0},{4,7},{5,6},{6,5},{7,4},{8,11},{9,10},{10,... | collective-permute-start | bytes 442376 | tf_op jit(solution)/shard_map/ppermute | solution.py:433
  6.5 11.8 %collective-permute-start = (bf16[576,128]{1,0:T(8,128)(2,1)S(1)}, bf16[576,128]{1,0:T(8,128)(2,1)S(1)}, u32[]{:S(2)}, u32[]{:S(2)}) collective-permute-start(bf16[576,128]{1,0:T(8,128)(2,1)S(1)} %get-tuple-element.61), channel_id=1, source_target_pairs={{0,1},{1,0},{2,3},{3,2},{4,5},{5,4},{6,7},{7,6},{8,9},{9,8},{10,11... | collective-permute-start | bytes 442376 | tf_op jit(solution)/shard_map/ppermute | solution.py:433
  6.7 11.6 %collective-permute-start.1 = (bf16[576,128]{1,0:T(8,128)(2,1)S(1)}, bf16[576,128]{1,0:T(8,128)(2,1)S(1)}, u32[]{:S(2)}, u32[]{:S(2)}) collective-permute-start(bf16[576,128]{1,0:T(8,128)(2,1)S(1)} %get-tuple-element.62), channel_id=1, source_target_pairs={{0,2},{1,3},{2,0},{3,1},{4,6},{5,7},{6,4},{7,5},{8,10},{9,11},{10,... | collective-permute-start | bytes 442376 | tf_op jit(solution)/shard_map/ppermute | solution.py:433
  8.6 10.1 %collective-permute-start.2 = (bf16[576,128]{1,0:T(8,128)(2,1)S(1)}, bf16[576,128]{1,0:T(8,128)(2,1)S(1)}, u32[]{:S(2)}, u32[]{:S(2)}) collective-permute-start(bf16[576,128]{1,0:T(8,128)(2,1)S(1)} %get-tuple-element.63), channel_id=1, source_target_pairs={{0,3},{1,2},{2,1},{3,0},{4,7},{5,6},{6,5},{7,4},{8,11},{9,10},{10,... | collective-permute-start | bytes 442376 | tf_op jit(solution)/shard_map/ppermute | solution.py:433
  16.0 9.3 %collective-permute-start.7 = (bf16[576,128]{1,0:T(8,128)(2,1)S(1)}, bf16[576,128]{1,0:T(8,128)(2,1)S(1)}, u32[]{:S(2)}, u32[]{:S(2)}) collective-permute-start(bf16[576,128]{1,0:T(8,128)(2,1)S(1)} %get-tuple-element.73), channel_id=1, source_target_pairs={{0,1},{1,0},{2,3},{3,2},{4,5},{5,4},{6,7},{7,6},{8,9},{9,8},{10,11... | collective-permute-start | bytes 442376 | tf_op jit(solution)/shard_map/ppermute | solution.py:433
  16.4 8.9 %collective-permute-start.8 = (bf16[576,128]{1,0:T(8,128)(2,1)S(1)}, bf16[576,128]{1,0:T(8,128)(2,1)S(1)}, u32[]{:S(2)}, u32[]{:S(2)}) collective-permute-start(bf16[576,128]{1,0:T(8,128)(2,1)S(1)} %get-tuple-element.74), channel_id=1, source_target_pairs={{0,2},{1,3},{2,0},{3,1},{4,6},{5,7},{6,4},{7,5},{8,10},{9,11},{10,... | collective-permute-start | bytes 442376 | tf_op jit(solution)/shard_map/ppermute | solution.py:433
  18.4 6.9 %collective-permute-start.9 = (bf16[576,128]{1,0:T(8,128)(2,1)S(1)}, bf16[576,128]{1,0:T(8,128)(2,1)S(1)}, u32[]{:S(2)}, u32[]{:S(2)}) collective-permute-start(bf16[576,128]{1,0:T(8,128)(2,1)S(1)} %get-tuple-element.75), channel_id=1, source_target_pairs={{0,3},{1,2},{2,1},{3,0},{4,7},{5,6},{6,5},{7,4},{8,11},{9,10},{10,... | collective-permute-start | bytes 442376 | tf_op jit(solution)/shard_map/ppermute | solution.py:433
  20.9 11.8 %copy-start.2 = (bf16[1,8,48,768]{3,2,1,0:T(8,128)(2,1)S(1)}, bf16[1,8,48,768]{3,2,1,0:T(8,128)(2,1)}, u32[]{:S(2)}) copy-start(bf16[1,8,48,768]{3,2,1,0:T(8,128)(2,1)} %grid_ref.6) | copy-start | bytes 1769476
  20.9 4.4 %collective-permute-start.6 = (bf16[288,128]{1,0:T(8,128)(2,1)S(1)}, bf16[288,128]{1,0:T(8,128)(2,1)S(1)}, u32[]{:S(2)}, u32[]{:S(2)}) collective-permute-start(bf16[288,128]{1,0:T(8,128)(2,1)S(1)} %get-tuple-element.85), channel_id=1, source_target_pairs={{0,4},{4,0},{8,12},{12,8},{16,20},{20,16},{24,28},{28,24},{1,5},{5... | collective-permute-start | bytes 221192 | tf_op jit(solution)/shard_map/ppermute | solution.py:433
  22.5 17.5 %copy-start.4 = (bf16[1,8,48,768]{3,2,1,0:T(8,128)(2,1)S(1)}, bf16[1,8,48,768]{3,2,1,0:T(8,128)(2,1)}, u32[]{:S(2)}) copy-start(bf16[1,8,48,768]{3,2,1,0:T(8,128)(2,1)} %grid_ref.7) | copy-start | bytes 1769476
  25.3 4.5 %collective-permute-start.10 = (bf16[288,128]{1,0:T(8,128)(2,1)S(1)}, bf16[288,128]{1,0:T(8,128)(2,1)S(1)}, u32[]{:S(2)}, u32[]{:S(2)}) collective-permute-start(bf16[288,128]{1,0:T(8,128)(2,1)S(1)} %add_convert_fusion.2), channel_id=1, source_target_pairs={{0,8},{4,12},{8,0},{12,4},{16,24},{20,28},{24,16},{28,20},{1,9},{5... | collective-permute-start | bytes 221192 | tf_op jit(solution)/shard_map/ppermute | solution.py:433
  27.2 8.3 %collective-permute-start.12 = (bf16[576,128]{1,0:T(8,128)(2,1)S(1)}, bf16[576,128]{1,0:T(8,128)(2,1)S(1)}, u32[]{:S(2)}, u32[]{:S(2)}) collective-permute-start(bf16[576,128]{1,0:T(8,128)(2,1)S(1)} %get-tuple-element.98), channel_id=1, source_target_pairs={{0,1},{1,0},{2,3},{3,2},{4,5},{5,4},{6,7},{7,6},{8,9},{9,8},{10,11... | collective-permute-start | bytes 442376 | tf_op jit(solution)/shard_map/ppermute | solution.py:433
  27.2 8.3 %collective-permute-start.13 = (bf16[576,128]{1,0:T(8,128)(2,1)S(1)}, bf16[576,128]{1,0:T(8,128)(2,1)S(1)}, u32[]{:S(2)}, u32[]{:S(2)}) collective-permute-start(bf16[576,128]{1,0:T(8,128)(2,1)S(1)} %get-tuple-element.99), channel_id=1, source_target_pairs={{0,2},{1,3},{2,0},{3,1},{4,6},{5,7},{6,4},{7,5},{8,10},{9,11},{10,... | collective-permute-start | bytes 442376 | tf_op jit(solution)/shard_map/ppermute | solution.py:433
  28.6 7.6 %collective-permute-start.14 = (bf16[576,128]{1,0:T(8,128)(2,1)S(1)}, bf16[576,128]{1,0:T(8,128)(2,1)S(1)}, u32[]{:S(2)}, u32[]{:S(2)}) collective-permute-start(bf16[576,128]{1,0:T(8,128)(2,1)S(1)} %get-tuple-element.100), channel_id=1, source_target_pairs={{0,3},{1,2},{2,1},{3,0},{4,7},{5,6},{6,5},{7,4},{8,11},{9,10},{10,... | collective-permute-start | bytes 442376 | tf_op jit(solution)/shard_map/ppermute | solution.py:433
  29.8 5.7 %collective-permute-start.11 = (bf16[288,128]{1,0:T(8,128)(2,1)S(1)}, bf16[288,128]{1,0:T(8,128)(2,1)S(1)}, u32[]{:S(2)}, u32[]{:S(2)}) collective-permute-start(bf16[288,128]{1,0:T(8,128)(2,1)S(1)} %add_convert_fusion.1), channel_id=1, source_target_pairs={{0,16},{4,20},{8,24},{12,28},{16,0},{20,4},{24,8},{28,12},{1,17},{... | collective-permute-start | bytes 221192 | tf_op jit(solution)/shard_map/ppermute | solution.py:433
  36.2 3.8 %collective-permute-start.16 = (bf16[288,128]{1,0:T(8,128)(2,1)S(1)}, bf16[288,128]{1,0:T(8,128)(2,1)S(1)}, u32[]{:S(2)}, u32[]{:S(2)}) collective-permute-start(bf16[288,128]{1,0:T(8,128)(2,1)S(1)} %add_convert_fusion.refs_0_), channel_id=1, source_target_pairs={{0,1},{1,0},{2,3},{3,2},{4,5},{5,4},{6,7},{7,6},{8,9},{9,8},{10,11... | collective-permute-start | bytes 221192 | tf_op jit(solution)/shard_map/ppermute | solution.py:433
  36.5 5.8 %collective-permute-start.15 = (bf16[288,128]{1,0:T(8,128)(2,1)S(1)}, bf16[288,128]{1,0:T(8,128)(2,1)S(1)}, u32[]{:S(2)}, u32[]{:S(2)}) collective-permute-start(bf16[288,128]{1,0:T(8,128)(2,1)S(1)} %add_convert_fusion.refs_0_), channel_id=1, source_target_pairs={{0,6},{1,7},{2,4},{3,5},{4,2},{5,3},{6,0},{7,1},{8,14},{9,15},{10,... | collective-permute-start | bytes 221192 | tf_op jit(solution)/shard_map/ppermute | solution.py:528
  38.9 4.6 %collective-permute-start.17 = (bf16[288,128]{1,0:T(8,128)(2,1)S(1)}, bf16[288,128]{1,0:T(8,128)(2,1)S(1)}, u32[]{:S(2)}, u32[]{:S(2)}) collective-permute-start(bf16[288,128]{1,0:T(8,128)(2,1)S(1)} %add_convert_fusion.refs_0_), channel_id=1, source_target_pairs={{0,4},{1,5},{2,6},{3,7},{4,0},{5,1},{6,2},{7,3},{8,12},{9,13},{10,... | collective-permute-start | bytes 221192 | tf_op jit(solution)/shard_map/ppermute | solution.py:528
  39.4 4.4 %collective-permute-start.19 = (bf16[288,128]{1,0:T(8,128)(2,1)S(1)}, bf16[288,128]{1,0:T(8,128)(2,1)S(1)}, u32[]{:S(2)}, u32[]{:S(2)}) collective-permute-start(bf16[288,128]{1,0:T(8,128)(2,1)S(1)} %add_convert_fusion.refs_0_), channel_id=1, source_target_pairs={{0,2},{1,3},{2,0},{3,1},{4,6},{5,7},{6,4},{7,5},{8,10},{9,11},{10,... | collective-permute-start | bytes 221192 | tf_op jit(solution)/shard_map/ppermute | solution.py:528
  42.3 1.7 %collective-permute-start.21 = (bf16[288,128]{1,0:T(8,128)(2,1)S(1)}, bf16[288,128]{1,0:T(8,128)(2,1)S(1)}, u32[]{:S(2)}, u32[]{:S(2)}) collective-permute-start(bf16[288,128]{1,0:T(8,128)(2,1)S(1)} %collective-permute-done.15.refs_5_), channel_id=1, source_target_pairs={{0,1},{1,0},{2,3},{3,2},{4,5},{5,4},{6,7},{7,6},{8,9},{9,8},{10,11... | collective-permute-start | bytes 221192 | tf_op jit(solution)/shard_map/ppermute | solution.py:433
  43.5 1.3 %collective-permute-start.18 = (bf16[288,128]{1,0:T(8,128)(2,1)S(1)}, bf16[288,128]{1,0:T(8,128)(2,1)S(1)}, u32[]{:S(2)}, u32[]{:S(2)}) collective-permute-start(bf16[288,128]{1,0:T(8,128)(2,1)S(1)} %collective-permute-done.17.refs_1_), channel_id=1, source_target_pairs={{0,1},{1,0},{2,3},{3,2},{4,5},{5,4},{6,7},{7,6},{8,9},{9,8},{10,11... | collective-permute-start | bytes 221192 | tf_op jit(solution)/shard_map/ppermute | solution.py:433
  43.8 1.3 %collective-permute-start.20 = (bf16[288,128]{1,0:T(8,128)(2,1)S(1)}, bf16[288,128]{1,0:T(8,128)(2,1)S(1)}, u32[]{:S(2)}, u32[]{:S(2)}) collective-permute-start(bf16[288,128]{1,0:T(8,128)(2,1)S(1)} %collective-permute-done.19.refs_4_), channel_id=1, source_target_pairs={{0,1},{1,0},{2,3},{3,2},{4,5},{5,4},{6,7},{7,6},{8,9},{9,8},{10,11... | collective-permute-start | bytes 221192 | tf_op jit(solution)/shard_map/ppermute | solution.py:433
  (4 other events, 7.2 us)
where the time goes:
time: 46.7 us; the launch traced here: 46.4 us
  starting transfers between devices  19.7 us (42%)
  Pallas kernels  11.9 us (25%)
  waiting for transfers between devices  9.26 us (20%)
  local copies, waits for them, and re-layouts  4.75 us (10%)
  between operations  0.76 us (2%)
    ppermute x19, starting transfers between devices, swap(): return lax.ppermute(value, axis, [(i, i ^ mask) for i in range(size)])  16.2 us
    pallas_call x10, Pallas kernels, call(): pl.pallas_call(kernel, out_shape=outs, in_specs=[HBM if i in in_hbm else...  11.9 us
    ppermute x19, waiting for transfers between devices, swap(): return lax.ppermute(value, axis, [(i, i ^ mask) for i in range(size)])  6.53 us
    unnamed x12, local copies, waits for them, and re-layouts  3.8 us
    ppermute x3, starting transfers between devices, by_groups(): lax.ppermute(grad, ('dp', 'lon'), pairs)  3.49 us
    ppermute x3, waiting for transfers between devices, by_groups(): lax.ppermute(grad, ('dp', 'lon'), pairs)  2.73 us
    dynamic_slice x1, local copies, waits for them, and re-layouts, own(): lax.dynamic_slice_in_dim(weight, lax.axis_index('lon') * 2, 2, axis=1)  0.96 us
  transfers between devices with their start and end apart: 22, of which 11 were waited for; matrix products, arithmetic and copies ran while one was open for 2% of the time, Pallas kernels for 22%

commit v1 on v0

--- a/solution.py
+++ b/solution.py
@@ -368,8 +368,9 @@
             pre_ref[parity, group] = pre
             terms[0][group] += dot(spec_t[group, :, span], pre)
             terms[1][group] += dot(act_t[group, :, span], dual)
-    whole = jnp.concatenate([weight_terms(terms[t][g], g) for t in range(2) for g in range(2)], axis=0)
-    grad_ref[...] = pack(whole.astype(BF)).reshape(grad_ref.shape)
+    for tensor in range(2):
+        both = [weight_terms(terms[tensor][group], group).astype(BF) for group in range(2)]
+        grad_ref[tensor] = pack(jnp.concatenate(both, axis=0))
     side = lax.axis_index("dp") % 2
     keep_ref[...] = grad_ref[side]
     send_ref[...] = grad_ref[1 - side]
@@ -385,44 +386,49 @@
     store_halves(lax.axis_index("lon"), outs, *results, even_ref, odd_ref)
 
 
-def spread_kernel(scale, *refs):
-    pieces, outs, whole, held, sems = refs[:8], refs[8:10], refs[10], refs[11], refs[12]
+def spread_kernel(scale, places, *refs):
+    count = len(places)
+    pieces, outs, held, sems = refs[:count], refs[-4:-2], refs[-2], refs[-1]
     me, side = lax.axis_index("lon"), lax.axis_index("dp") % 2
     width = held.shape[-1]
-    copies = []
-    for slot in (0, 1, 2, 3):
-        source = me ^ slot
-        whole[side] = pieces[2 * slot][...]
-        whole[1 - side] = pieces[2 * slot + 1][...]
-        rows = unpack(whole[...].reshape(-1, whole.shape[-1])).astype(F32) * scale
+
+    def each_copy(index, act):
+        mask, other = places[index]
         for tensor in range(2):
-            for group in range(2):
-                start = (tensor * 2 + group) * width
-                block = rows[start : start + width]
-                held[slot, tensor, 0, group] = block[:, :width]
-                held[slot, tensor, 1, group] = block[:, width:]
-            copy = pltpu.make_async_copy(
-                held.at[slot, tensor],
-                outs[tensor].at[:, pl.ds(2 * source, 2)],
-                sems.at[slot, tensor],
-            )
-            copy.start()
-            copies.append(copy)
-    for copy in copies:
-        copy.wait()
+
+            @pl.when((side ^ other) == tensor)
+            def _():
+                act(
+                    pltpu.make_async_copy(
+                        held.at[index],
+                        outs[tensor].at[:, pl.ds(2 * (me ^ mask), 2)],
+                        sems.at[index],
+                    )
+                )
+
+    for index in range(count):
+        rows = unpack(pieces[index][...]).astype(F32) * scale
+        for group in range(2):
+            block = rows[group * width : (group + 1) * width]
+            held[index, 0, group] = block[:, :width]
+            held[index, 1, group] = block[:, width:]
+        each_copy(index, lambda copy: copy.start())
+    for index in range(count):
+        each_copy(index, lambda copy: copy.wait())
 
 
 VMEM = pl.BlockSpec(memory_space=pltpu.VMEM)
 HBM = pl.BlockSpec(memory_space=pltpu.HBM)
 
 
-def call(kernel, outs, args, scratch=(), in_hbm=(), out_hbm=False, vmem_mib=20):
+def call(kernel, outs, args, scratch=(), in_hbm=(), out_hbm=False, aliases=None, vmem_mib=20):
     return pl.pallas_call(
         kernel,
         out_shape=outs,
-        in_specs=[HBM if i in in_hbm else VMEM for i in range(len(args))],
+        in_specs=[HBM if i in in_hbm or i in (aliases or {}) else VMEM for i in range(len(args))],
         out_specs=[HBM if out_hbm else VMEM] * len(outs),
         scratch_shapes=scratch,
+        input_output_aliases=aliases or {},
         compiler_params=pltpu.CompilerParams(vmem_limit_bytes=vmem_mib * 2**20),
         cost_estimate=pl.CostEstimate(flops=1, bytes_accessed=1, transcendentals=0),
     )(*args)
@@ -515,31 +521,39 @@
     while mask < sample_count:
         other = swap(grad, "dp", mask)
         if mask == 4:
-            other, layer_out, pull_slots = after(other, layer_out, pull_slots)
+            other, layer_out, pull_slots[1:3] = after(other, layer_out, pull_slots[1:3])
         grad = added(grad, other)
         mask *= 2
     beside = swap(grad, "lon", 1)
-    beside, pull_slots = after(beside, pull_slots)
     (field_grad,) = call(merge_kernel, [grid_shape], [cotangent, *pull_slots])
-    pieces = []
-    for lon_mask in (0, 2):
-        for dp_mask in (0, 1):
-            pairs = flip_pairs(sample_count, lon_count, dp_mask, lon_mask)
-            pieces.append(lax.ppermute(grad, ("dp", "lon"), pairs) if dp_mask + lon_mask else grad)
-    pieces[3], field_grad = after(pieces[3], field_grad)
-    across = [beside] + [swap(p, "lon", 1) for p in pieces[1:]]
-    ordered = pieces[:2] + across[:2] + pieces[2:] + across[2:]
+    across, flipped, corner = (
+        lax.ppermute(grad, ("dp", "lon"), flip_pairs(sample_count, lon_count, d, i))
+        for d, i in ((0, 2), (1, 0), (1, 2))
+    )
+    beside, corner, field_grad = after(beside, corner, field_grad)
     grad_shape = jax.ShapeDtypeStruct(first_weight.shape, F32)
-    first_grad, second_grad = call(
-        functools.partial(spread_kernel, 1.0 / sample_count),
-        [grad_shape] * 2,
-        ordered,
-        [
-            pltpu.VMEM((2, *piece.shape), BF),
-            pltpu.VMEM((4, 2, 2, 2, group_width, group_width), F32),
-            pltpu.SemaphoreType.DMA((4, 2)),
-        ],
-        out_hbm=True,
+
+    def spread(places, pieces, outs=()):
+        return call(
+            functools.partial(spread_kernel, 1.0 / sample_count, places),
+            [grad_shape] * 2,
+            [*pieces, *outs],
+            [
+                pltpu.VMEM((len(places), 2, 2, group_width, group_width), F32),
+                pltpu.SemaphoreType.DMA((len(places),)),
+            ],
+            out_hbm=True,
+            aliases={len(pieces) + i: i for i in range(len(outs))},
+        )
+
+    corner_core = swap(corner, "lon", 1)
+    early = spread(((2, 1), (0, 0), (1, 0)), [corner, grad, beside])
+    across, *early = after(across, *early)
+    across_core, flipped_core = swap(across, "lon", 1), swap(flipped, "lon", 1)
+    first_grad, second_grad = spread(
+        ((3, 1), (2, 0), (0, 1), (3, 0), (1, 1)),
+        [corner_core, across, flipped, across_core, flipped_core],
+        early,
     )
     return layer_out, field_grad, first_grad, second_grad
 

time: 46.7 us -> 45.6 us (0.976)
  waiting for transfers between devices: 9.26 us -> 7.67 us
  Pallas kernels: 11.9 us -> 12.8 us
    ppermute x3, waiting for transfers between devices: 2.73 us -> 1.79 us  [by_groups(): lax.ppermute(grad, ('dp', 'lon'), flip_pairs(sample_count, lon_count, d, i))]
    pallas_call x10 -> x11, Pallas kernels: 11.9 us -> 12.8 us  [call(): pl.pallas_call(kernel, out_shape=outs, in_specs=[HBM if i in in_hbm or i...]
    ppermute x19, waiting for transfers between devices: 6.53 us -> 5.88 us  [swap(): return lax.ppermute(value, axis, [(i, i ^ mask) for i in range(size)])]
  transfers between devices with their start and end apart: 22 -> 22, of which waited for: 11 -> 10; matrix products, arithmetic and copies ran while one was open for 2% -> 2% of each run, Pallas kernels for 22% -> 25%
where the time goes in v1:
time: 45.6 us; the launch traced here: 45.3 us
  starting transfers between devices  19.3 us (42%)
  Pallas kernels  12.8 us (28%)
  waiting for transfers between devices  7.67 us (17%)
  local copies, waits for them, and re-layouts  4.75 us (10%)
  between operations  0.76 us (2%)
    ppermute x19, starting transfers between devices, swap(): return lax.ppermute(value, axis, [(i, i ^ mask) for i in range(size)])  15.8 us
    pallas_call x11, Pallas kernels, call(): pl.pallas_call(kernel, out_shape=outs, in_specs=[HBM if i in in_hbm or i...  12.8 us
    ppermute x19, waiting for transfers between devices, swap(): return lax.ppermute(value, axis, [(i, i ^ mask) for i in range(size)])  5.88 us
    unnamed x12, local copies, waits for them, and re-layouts  3.8 us
    ppermute x3, starting transfers between devices, by_groups(): lax.ppermute(grad, ('dp', 'lon'), flip_pairs(sample_count, lon_count, d, i))  3.49 us
    ppermute x3, waiting for transfers between devices, by_groups(): lax.ppermute(grad, ('dp', 'lon'), flip_pairs(sample_count, lon_count, d, i))  1.79 us
    dynamic_slice x1, local copies, waits for them, and re-layouts, own(): lax.dynamic_slice_in_dim(weight, lax.axis_index('lon') * 2, 2, axis=1)  0.96 us
  transfers between devices with their start and end apart: 22, of which 10 were waited for; matrix products, arithmetic and copies ran while one was open for 2% of the time, Pallas kernels for 25%

profile of v1, /device:TPU:0, one launch (start us, length us, event | category | flops | bytes accessed | tf_op | source)
XLA Modules:
  0.0 45.3 jit_solution(8674053715002851683)
XLA Ops:
  0.6 1.1 %copy-done.1 = bf16[1,8,48,768]{3,2,1,0:T(8,128)(2,1)S(1)} copy-done((bf16[1,8,48,768]{3,2,1,0:T(8,128)(2,1)S(1)}, bf16[1,8,48,768]{3,2,1,0:T(8,128)(2,1)}, u32[]{:S(2)}) %copy-start.1) | copy-done | bytes 589848
  2.5 2.6 %collective-permute-start.4 = (bf16[576,128]{1,0:T(8,128)(2,1)S(1)}, bf16[576,128]{1,0:T(8,128)(2,1)S(1)}, u32[]{:S(2)}, u32[]{:S(2)}) collective-permute-start(bf16[576,128]{1,0:T(8,128)(2,1)S(1)} %get-tuple-element.65), channel_id=1, source_target_pairs={{0,2},{1,3},{2,0},{3,1},{4,6},{5,7},{6,4},{7,5},{8,10},{9,11},{10,... | collective-permute-start | bytes 442376 | tf_op jit(solution)/shard_map/ppermute | solution.py:439
  5.2 1.1 %copy-done.3 = bf16[1,8,48,768]{3,2,1,0:T(8,128)(2,1)S(1)} copy-done((bf16[1,8,48,768]{3,2,1,0:T(8,128)(2,1)S(1)}, bf16[1,8,48,768]{3,2,1,0:T(8,128)(2,1)}, u32[]{:S(2)}) %copy-start.3) | copy-done | bytes 589848
  6.7 1.9 %collective-permute-start.1 = (bf16[576,128]{1,0:T(8,128)(2,1)S(1)}, bf16[576,128]{1,0:T(8,128)(2,1)S(1)}, u32[]{:S(2)}, u32[]{:S(2)}) collective-permute-start(bf16[576,128]{1,0:T(8,128)(2,1)S(1)} %get-tuple-element.61), channel_id=1, source_target_pairs={{0,2},{1,3},{2,0},{3,1},{4,6},{5,7},{6,4},{7,5},{8,10},{9,11},{10,... | collective-permute-start | bytes 442376 | tf_op jit(solution)/shard_map/ppermute | solution.py:439
  8.6 1.0 %constant_dynamic-slice_fusion = (bf16[2,2,96,96]{3,2,1,0:T(8,128)(2,1)S(1)}, bf16[2,2,96,96]{3,2,1,0:T(8,128)(2,1)S(1)}) fusion(bf16[2,8,96,96]{3,2,1,0:T(8,128)(2,1)} %param.9, s32[]{:T(128)S(6)} %select_n.4, bf16[2,8,96,96]{3,2,1,0:T(8,128)(2,1)} %param.8), kind=kLoop, calls=%fused_computation.3 | loop fusion | bytes 294916 | tf_op jit(solution)/shard_map/dynamic_slice | solution.py:476
  9.6 1.7 %copy-done.5 = bf16[2,768,768]{2,1,0:T(8,128)(2,1)S(1)} copy-done((bf16[2,768,768]{2,1,0:T(8,128)(2,1)S(1)}, bf16[2,768,768]{2,1,0:T(8,128)(2,1)}, u32[]{:S(2)}) %copy-start.5) | copy-done | bytes 2359320
  12.4 2.2 %shard_map.96 = (bf16[2,2,384,192]{3,2,1,0:T(8,128)(2,1)S(1)}, f32[2,2,384,192]{3,2,1,0:T(8,128)S(1)}, bf16[2,192,768]{2,1,0:T(8,128)(2,1)S(1)}, bf16[2,192,768]{2,1,0:T(8,128)(2,1)S(1)}) custom-call(bf16[576,128]{1,0:T(8,128)(2,1)S(1)} %get-tuple-element.63.refs_0_, bf16[576,128]{1,0:T(8,128)(2,1)S(1)} %collective-permute-done.3.refs_1_, ...), custom_call_target="tpu_custom_call" | custom-call | flops 1 | bytes 1 | tf_op jit(solution)/shard_map/pallas_call | solution.py:425
  14.6 1.4 %shard_map.97 = (bf16[576,128]{1,0:T(8,128)(2,1)S(1)}, bf16[576,128]{1,0:T(8,128)(2,1)S(1)}, bf16[576,128]{1,0:T(8,128)(2,1)S(1)}, bf16[576,128]{1,0:T(8,128)(2,1)S(1)}) custom-call(bf16[2,2,384,192]{3,2,1,0:T(8,128)(2,1)S(1)} %get-tuple-element.69.act_ref, bf16[2,768,768]{2,1,0:T(8,128)(2,1)S(1)} %copy-done, ...), custom_call_target="tpu_custom_call" | custom-call | flops 1 | bytes 1 | tf_op jit(solution)/shard_map/pallas_call | solution.py:425
  16.4 1.9 %collective-permute-start.8 = (bf16[576,128]{1,0:T(8,128)(2,1)S(1)}, bf16[576,128]{1,0:T(8,128)(2,1)S(1)}, u32[]{:S(2)}, u32[]{:S(2)}) collective-permute-start(bf16[576,128]{1,0:T(8,128)(2,1)S(1)} %get-tuple-element.73), channel_id=1, source_target_pairs={{0,2},{1,3},{2,0},{3,1},{4,6},{5,7},{6,4},{7,5},{8,10},{9,11},{10,... | collective-permute-start | bytes 442376 | tf_op jit(solution)/shard_map/ppermute | solution.py:439
  18.7 2.2 %shard_map.98 = (bf16[2,2,384,192]{3,2,1,0:T(8,128)(2,1)S(1)}, bf16[288,128]{1,0:T(8,128)(2,1)S(1)}, bf16[288,128]{1,0:T(8,128)(2,1)S(1)}) custom-call(bf16[576,128]{1,0:T(8,128)(2,1)S(1)} %get-tuple-element.75.refs_0_, bf16[576,128]{1,0:T(8,128)(2,1)S(1)} %collective-permute-done.refs_1_, bf16[576,128]{1,0:T(8,128)(2,1)S(1)} %collective-permute-done.1.refs_2_, ...), custom_call_target="tpu_custom_call" | custom-call | flops 1 | bytes 1 | tf_op jit(solution)/shard_map/pallas_call | solution.py:425
  20.9 1.6 %collective-permute-start.6 = (bf16[288,128]{1,0:T(8,128)(2,1)S(1)}, bf16[288,128]{1,0:T(8,128)(2,1)S(1)}, u32[]{:S(2)}, u32[]{:S(2)}) collective-permute-start(bf16[288,128]{1,0:T(8,128)(2,1)S(1)} %get-tuple-element.84), channel_id=1, source_target_pairs={{0,4},{4,0},{8,12},{12,8},{16,20},{20,16},{24,28},{28,24},{1,5},{5... | collective-permute-start | bytes 221192 | tf_op jit(solution)/shard_map/ppermute | solution.py:439
  22.6 1.3 %shard_map.99 = (bf16[576,128]{1,0:T(8,128)(2,1)S(1)}, bf16[576,128]{1,0:T(8,128)(2,1)S(1)}, bf16[576,128]{1,0:T(8,128)(2,1)S(1)}, bf16[576,128]{1,0:T(8,128)(2,1)S(1)}) custom-call(bf16[2,2,384,192]{3,2,1,0:T(8,128)(2,1)S(1)} %get-tuple-element.85.pre_ref, bf16[2,768,768]{2,1,0:T(8,128)(2,1)S(1)} %copy-done, ...), custom_call_target="tpu_custom_call" | custom-call | flops 1 | bytes 1 | tf_op jit(solution)/shard_map/pallas_call | solution.py:425
  23.9 1.5 %collective-permute-done.6 = bf16[288,128]{1,0:T(8,128)(2,1)S(1)} collective-permute-done((bf16[288,128]{1,0:T(8,128)(2,1)S(1)}, bf16[288,128]{1,0:T(8,128)(2,1)S(1)}, u32[]{:S(2)}, u32[]{:S(2)}) %collective-permute-start.6) | collective-permute-done | bytes 73760 | tf_op jit(solution)/shard_map/ppermute | solution.py:439
  25.4 1.8 %collective-permute-start.10 = (bf16[288,128]{1,0:T(8,128)(2,1)S(1)}, bf16[288,128]{1,0:T(8,128)(2,1)S(1)}, u32[]{:S(2)}, u32[]{:S(2)}) collective-permute-start(bf16[288,128]{1,0:T(8,128)(2,1)S(1)} %add_convert_fusion.2), channel_id=1, source_target_pairs={{0,8},{4,12},{8,0},{12,4},{16,24},{20,28},{24,16},{28,20},{1,9},{5... | collective-permute-start | bytes 221192 | tf_op jit(solution)/shard_map/ppermute | solution.py:439
  27.2 1.5 %collective-permute-start.13 = (bf16[576,128]{1,0:T(8,128)(2,1)S(1)}, bf16[576,128]{1,0:T(8,128)(2,1)S(1)}, u32[]{:S(2)}, u32[]{:S(2)}) collective-permute-start(bf16[576,128]{1,0:T(8,128)(2,1)S(1)} %get-tuple-element.97), channel_id=1, source_target_pairs={{0,2},{1,3},{2,0},{3,1},{4,6},{5,7},{6,4},{7,5},{8,10},{9,11},{10,... | collective-permute-start | bytes 442376 | tf_op jit(solution)/shard_map/ppermute | solution.py:439
  28.7 1.1 %collective-permute-done.10 = bf16[288,128]{1,0:T(8,128)(2,1)S(1)} collective-permute-done((bf16[288,128]{1,0:T(8,128)(2,1)S(1)}, bf16[288,128]{1,0:T(8,128)(2,1)S(1)}, u32[]{:S(2)}, u32[]{:S(2)}) %collective-permute-start.10) | collective-permute-done | bytes 73760 | tf_op jit(solution)/shard_map/ppermute | solution.py:439
  29.8 2.8 %collective-permute-start.11 = (bf16[288,128]{1,0:T(8,128)(2,1)S(1)}, bf16[288,128]{1,0:T(8,128)(2,1)S(1)}, u32[]{:S(2)}, u32[]{:S(2)}) collective-permute-start(bf16[288,128]{1,0:T(8,128)(2,1)S(1)} %add_convert_fusion.1), channel_id=1, source_target_pairs={{0,16},{4,20},{8,24},{12,28},{16,0},{20,4},{24,8},{28,12},{1,17},{... | collective-permute-start | bytes 221192 | tf_op jit(solution)/shard_map/ppermute | solution.py:439
  32.7 1.1 %shard_map.100 = bf16[1,8,48,768]{3,2,1,0:T(8,128)(2,1)} custom-call(bf16[1,8,48,768]{3,2,1,0:T(8,128)(2,1)S(1)} %copy-done.2, bf16[576,128]{1,0:T(8,128)(2,1)S(1)} %get-tuple-element.92.refs_0_, bf16[576,128]{1,0:T(8,128)(2,1)S(1)} %collective-permute-done.7.refs_1_, bf16[576,128]{1,0:T(8,128)(2,1)S(1)} %collective-permute-done.8.refs_2_, ...), custom_call_target="tpu_custom_call" | custom-call | flops 1 | bytes 1 | tf_op jit(solution)/shard_map/pallas_call | solution.py:425
  33.7 1.4 %collective-permute-done.11 = bf16[288,128]{1,0:T(8,128)(2,1)S(1)} collective-permute-done((bf16[288,128]{1,0:T(8,128)(2,1)S(1)}, bf16[288,128]{1,0:T(8,128)(2,1)S(1)}, u32[]{:S(2)}, u32[]{:S(2)}) %collective-permute-start.11) | collective-permute-done | bytes 73760 | tf_op jit(solution)/shard_map/ppermute | solution.py:439
  35.4 2.5 %collective-permute-start.15 = (bf16[288,128]{1,0:T(8,128)(2,1)S(1)}, bf16[288,128]{1,0:T(8,128)(2,1)S(1)}, u32[]{:S(2)}, u32[]{:S(2)}) collective-permute-start(bf16[288,128]{1,0:T(8,128)(2,1)S(1)} %add_convert_fusion.refs_1_), channel_id=1, source_target_pairs={{0,6},{1,7},{2,4},{3,5},{4,2},{5,3},{6,0},{7,1},{8,14},{9,15},{10,... | collective-permute-start | bytes 221192 | tf_op jit(solution)/shard_map/ppermute | solution.py:530
  38.9 1.1 %shard_map.101 = bf16[1,8,48,768]{3,2,1,0:T(8,128)(2,1)} custom-call(bf16[1,8,48,768]{3,2,1,0:T(8,128)(2,1)S(1)} %copy-done.4, bf16[576,128]{1,0:T(8,128)(2,1)S(1)} %get-tuple-element.100.refs_0_, bf16[576,128]{1,0:T(8,128)(2,1)S(1)} %collective-permute-done.12.refs_1_, bf16[576,128]{1,0:T(8,128)(2,1)S(1)} %collective-permute-done.13.refs_2_, ...), custom_call_target="tpu_custom_call" | custom-call | flops 1 | bytes 1 | tf_op jit(solution)/shard_map/pallas_call | solution.py:425
  40.0 0.9 %collective-permute-done.15.refs_0_ = bf16[288,128]{1,0:T(8,128)(2,1)S(1)} collective-permute-done((bf16[288,128]{1,0:T(8,128)(2,1)S(1)}, bf16[288,128]{1,0:T(8,128)(2,1)S(1)}, u32[]{:S(2)}, u32[]{:S(2)}) %collective-permute-start.15) | collective-permute-done | bytes 73760 | tf_op jit(solution)/shard_map/ppermute | solution.py:530
  40.9 1.0 %shard_map.102 = (f32[2,8,96,96]{3,2,1,0:T(8,128)}, f32[2,8,96,96]{3,2,1,0:T(8,128)}) custom-call(bf16[288,128]{1,0:T(8,128)(2,1)S(1)} %collective-permute-done.15.refs_0_, bf16[288,128]{1,0:T(8,128)(2,1)S(1)} %add_convert_fusion.refs_1_, bf16[288,128]{1,0:T(8,128)(2,1)S(1)} %collective-permute-done.14.refs_2_), custom_call_target="tpu_custom_call" | custom-call | flops 1 | bytes 1 | tf_op jit(solution)/shard_map/pallas_call | solution.py:425
  44.1 1.2 %shard_map.103 = (f32[2,8,96,96]{3,2,1,0:T(8,128)}, f32[2,8,96,96]{3,2,1,0:T(8,128)}) custom-call(bf16[288,128]{1,0:T(8,128)(2,1)S(1)} %collective-permute-done.17.refs_0_, bf16[288,128]{1,0:T(8,128)(2,1)S(1)} %collective-permute-done.18.refs_1_, bf16[288,128]{1,0:T(8,128)(2,1)S(1)} %collective-permute-done.19.refs_2_, ...), custom_call_target="tpu_custom_call", output_to_operand_aliasing={{0}: (5, {}), {1}: (6, {})} | custom-call | flops 1 | bytes 1 | tf_op jit(solution)/shard_map/pallas_call | solution.py:425
  (47 shorter events, 7.0 us)
Async XLA Ops:
  2.0 6.6 %collective-permute-start.3 = (bf16[576,128]{1,0:T(8,128)(2,1)S(1)}, bf16[576,128]{1,0:T(8,128)(2,1)S(1)}, u32[]{:S(2)}, u32[]{:S(2)}) collective-permute-start(bf16[576,128]{1,0:T(8,128)(2,1)S(1)} %get-tuple-element.64), channel_id=1, source_target_pairs={{0,1},{1,0},{2,3},{3,2},{4,5},{5,4},{6,7},{7,6},{8,9},{9,8},{10,11... | collective-permute-start | bytes 442376 | tf_op jit(solution)/shard_map/ppermute | solution.py:439
  2.5 9.5 %collective-permute-start.4 = (bf16[576,128]{1,0:T(8,128)(2,1)S(1)}, bf16[576,128]{1,0:T(8,128)(2,1)S(1)}, u32[]{:S(2)}, u32[]{:S(2)}) collective-permute-start(bf16[576,128]{1,0:T(8,128)(2,1)S(1)} %get-tuple-element.65), channel_id=1, source_target_pairs={{0,2},{1,3},{2,0},{3,1},{4,6},{5,7},{6,4},{7,5},{8,10},{9,11},{10,... | collective-permute-start | bytes 442376 | tf_op jit(solution)/shard_map/ppermute | solution.py:439
  5.1 7.3 %collective-permute-start.5 = (bf16[576,128]{1,0:T(8,128)(2,1)S(1)}, bf16[576,128]{1,0:T(8,128)(2,1)S(1)}, u32[]{:S(2)}, u32[]{:S(2)}) collective-permute-start(bf16[576,128]{1,0:T(8,128)(2,1)S(1)} %get-tuple-element.66), channel_id=1, source_target_pairs={{0,3},{1,2},{2,1},{3,0},{4,7},{5,6},{6,5},{7,4},{8,11},{9,10},{10,... | collective-permute-start | bytes 442376 | tf_op jit(solution)/shard_map/ppermute | solution.py:439
  6.5 11.8 %collective-permute-start = (bf16[576,128]{1,0:T(8,128)(2,1)S(1)}, bf16[576,128]{1,0:T(8,128)(2,1)S(1)}, u32[]{:S(2)}, u32[]{:S(2)}) collective-permute-start(bf16[576,128]{1,0:T(8,128)(2,1)S(1)} %get-tuple-element.60), channel_id=1, source_target_pairs={{0,1},{1,0},{2,3},{3,2},{4,5},{5,4},{6,7},{7,6},{8,9},{9,8},{10,11... | collective-permute-start | bytes 442376 | tf_op jit(solution)/shard_map/ppermute | solution.py:439
  6.7 11.6 %collective-permute-start.1 = (bf16[576,128]{1,0:T(8,128)(2,1)S(1)}, bf16[576,128]{1,0:T(8,128)(2,1)S(1)}, u32[]{:S(2)}, u32[]{:S(2)}) collective-permute-start(bf16[576,128]{1,0:T(8,128)(2,1)S(1)} %get-tuple-element.61), channel_id=1, source_target_pairs={{0,2},{1,3},{2,0},{3,1},{4,6},{5,7},{6,4},{7,5},{8,10},{9,11},{10,... | collective-permute-start | bytes 442376 | tf_op jit(solution)/shard_map/ppermute | solution.py:439
  8.6 10.1 %collective-permute-start.2 = (bf16[576,128]{1,0:T(8,128)(2,1)S(1)}, bf16[576,128]{1,0:T(8,128)(2,1)S(1)}, u32[]{:S(2)}, u32[]{:S(2)}) collective-permute-start(bf16[576,128]{1,0:T(8,128)(2,1)S(1)} %get-tuple-element.62), channel_id=1, source_target_pairs={{0,3},{1,2},{2,1},{3,0},{4,7},{5,6},{6,5},{7,4},{8,11},{9,10},{10,... | collective-permute-start | bytes 442376 | tf_op jit(solution)/shard_map/ppermute | solution.py:439
  16.0 9.4 %collective-permute-start.7 = (bf16[576,128]{1,0:T(8,128)(2,1)S(1)}, bf16[576,128]{1,0:T(8,128)(2,1)S(1)}, u32[]{:S(2)}, u32[]{:S(2)}) collective-permute-start(bf16[576,128]{1,0:T(8,128)(2,1)S(1)} %get-tuple-element.72), channel_id=1, source_target_pairs={{0,1},{1,0},{2,3},{3,2},{4,5},{5,4},{6,7},{7,6},{8,9},{9,8},{10,11... | collective-permute-start | bytes 442376 | tf_op jit(solution)/shard_map/ppermute | solution.py:439
  16.4 9.0 %collective-permute-start.8 = (bf16[576,128]{1,0:T(8,128)(2,1)S(1)}, bf16[576,128]{1,0:T(8,128)(2,1)S(1)}, u32[]{:S(2)}, u32[]{:S(2)}) collective-permute-start(bf16[576,128]{1,0:T(8,128)(2,1)S(1)} %get-tuple-element.73), channel_id=1, source_target_pairs={{0,2},{1,3},{2,0},{3,1},{4,6},{5,7},{6,4},{7,5},{8,10},{9,11},{10,... | collective-permute-start | bytes 442376 | tf_op jit(solution)/shard_map/ppermute | solution.py:439
  18.4 7.0 %collective-permute-start.9 = (bf16[576,128]{1,0:T(8,128)(2,1)S(1)}, bf16[576,128]{1,0:T(8,128)(2,1)S(1)}, u32[]{:S(2)}, u32[]{:S(2)}) collective-permute-start(bf16[576,128]{1,0:T(8,128)(2,1)S(1)} %get-tuple-element.74), channel_id=1, source_target_pairs={{0,3},{1,2},{2,1},{3,0},{4,7},{5,6},{6,5},{7,4},{8,11},{9,10},{10,... | collective-permute-start | bytes 442376 | tf_op jit(solution)/shard_map/ppermute | solution.py:439
  20.9 11.8 %copy-start.2 = (bf16[1,8,48,768]{3,2,1,0:T(8,128)(2,1)S(1)}, bf16[1,8,48,768]{3,2,1,0:T(8,128)(2,1)}, u32[]{:S(2)}) copy-start(bf16[1,8,48,768]{3,2,1,0:T(8,128)(2,1)} %grid_ref.6) | copy-start | bytes 1769476
  20.9 4.4 %collective-permute-start.6 = (bf16[288,128]{1,0:T(8,128)(2,1)S(1)}, bf16[288,128]{1,0:T(8,128)(2,1)S(1)}, u32[]{:S(2)}, u32[]{:S(2)}) collective-permute-start(bf16[288,128]{1,0:T(8,128)(2,1)S(1)} %get-tuple-element.84), channel_id=1, source_target_pairs={{0,4},{4,0},{8,12},{12,8},{16,20},{20,16},{24,28},{28,24},{1,5},{5... | collective-permute-start | bytes 221192 | tf_op jit(solution)/shard_map/ppermute | solution.py:439
  22.6 16.4 %copy-start.4 = (bf16[1,8,48,768]{3,2,1,0:T(8,128)(2,1)S(1)}, bf16[1,8,48,768]{3,2,1,0:T(8,128)(2,1)}, u32[]{:S(2)}) copy-start(bf16[1,8,48,768]{3,2,1,0:T(8,128)(2,1)} %grid_ref.7) | copy-start | bytes 1769476
  25.4 4.4 %collective-permute-start.10 = (bf16[288,128]{1,0:T(8,128)(2,1)S(1)}, bf16[288,128]{1,0:T(8,128)(2,1)S(1)}, u32[]{:S(2)}, u32[]{:S(2)}) collective-permute-start(bf16[288,128]{1,0:T(8,128)(2,1)S(1)} %add_convert_fusion.2), channel_id=1, source_target_pairs={{0,8},{4,12},{8,0},{12,4},{16,24},{20,28},{24,16},{28,20},{1,9},{5... | collective-permute-start | bytes 221192 | tf_op jit(solution)/shard_map/ppermute | solution.py:439
  27.2 7.9 %collective-permute-start.12 = (bf16[576,128]{1,0:T(8,128)(2,1)S(1)}, bf16[576,128]{1,0:T(8,128)(2,1)S(1)}, u32[]{:S(2)}, u32[]{:S(2)}) collective-permute-start(bf16[576,128]{1,0:T(8,128)(2,1)S(1)} %get-tuple-element.96), channel_id=1, source_target_pairs={{0,1},{1,0},{2,3},{3,2},{4,5},{5,4},{6,7},{7,6},{8,9},{9,8},{10,11... | collective-permute-start | bytes 442376 | tf_op jit(solution)/shard_map/ppermute | solution.py:439
  27.2 7.9 %collective-permute-start.13 = (bf16[576,128]{1,0:T(8,128)(2,1)S(1)}, bf16[576,128]{1,0:T(8,128)(2,1)S(1)}, u32[]{:S(2)}, u32[]{:S(2)}) collective-permute-start(bf16[576,128]{1,0:T(8,128)(2,1)S(1)} %get-tuple-element.97), channel_id=1, source_target_pairs={{0,2},{1,3},{2,0},{3,1},{4,6},{5,7},{6,4},{7,5},{8,10},{9,11},{10,... | collective-permute-start | bytes 442376 | tf_op jit(solution)/shard_map/ppermute | solution.py:439
  29.8 5.3 %collective-permute-start.11 = (bf16[288,128]{1,0:T(8,128)(2,1)S(1)}, bf16[288,128]{1,0:T(8,128)(2,1)S(1)}, u32[]{:S(2)}, u32[]{:S(2)}) collective-permute-start(bf16[288,128]{1,0:T(8,128)(2,1)S(1)} %add_convert_fusion.1), channel_id=1, source_target_pairs={{0,16},{4,20},{8,24},{12,28},{16,0},{20,4},{24,8},{28,12},{1,17},{... | collective-permute-start | bytes 221192 | tf_op jit(solution)/shard_map/ppermute | solution.py:439
  32.7 6.3 %collective-permute-start.16 = (bf16[576,128]{1,0:T(8,128)(2,1)S(1)}, bf16[576,128]{1,0:T(8,128)(2,1)S(1)}, u32[]{:S(2)}, u32[]{:S(2)}) collective-permute-start(bf16[576,128]{1,0:T(8,128)(2,1)S(1)} %get-tuple-element.103), channel_id=1, source_target_pairs={{0,3},{1,2},{2,1},{3,0},{4,7},{5,6},{6,5},{7,4},{8,11},{9,10},{10,... | collective-permute-start | bytes 442376 | tf_op jit(solution)/shard_map/ppermute | solution.py:439
  35.2 4.8 %collective-permute-start.14 = (bf16[288,128]{1,0:T(8,128)(2,1)S(1)}, bf16[288,128]{1,0:T(8,128)(2,1)S(1)}, u32[]{:S(2)}, u32[]{:S(2)}) collective-permute-start(bf16[288,128]{1,0:T(8,128)(2,1)S(1)} %add_convert_fusion.refs_1_), channel_id=1, source_target_pairs={{0,1},{1,0},{2,3},{3,2},{4,5},{5,4},{6,7},{7,6},{8,9},{9,8},{10,11... | collective-permute-start | bytes 221192 | tf_op jit(solution)/shard_map/ppermute | solution.py:439
  35.4 5.4 %collective-permute-start.15 = (bf16[288,128]{1,0:T(8,128)(2,1)S(1)}, bf16[288,128]{1,0:T(8,128)(2,1)S(1)}, u32[]{:S(2)}, u32[]{:S(2)}) collective-permute-start(bf16[288,128]{1,0:T(8,128)(2,1)S(1)} %add_convert_fusion.refs_1_), channel_id=1, source_target_pairs={{0,6},{1,7},{2,4},{3,5},{4,2},{5,3},{6,0},{7,1},{8,14},{9,15},{10,... | collective-permute-start | bytes 221192 | tf_op jit(solution)/shard_map/ppermute | solution.py:530
  37.9 4.5 %collective-permute-start.18 = (bf16[288,128]{1,0:T(8,128)(2,1)S(1)}, bf16[288,128]{1,0:T(8,128)(2,1)S(1)}, u32[]{:S(2)}, u32[]{:S(2)}) collective-permute-start(bf16[288,128]{1,0:T(8,128)(2,1)S(1)} %add_convert_fusion.refs_1_), channel_id=1, source_target_pairs={{0,2},{1,3},{2,0},{3,1},{4,6},{5,7},{6,4},{7,5},{8,10},{9,11},{10,... | collective-permute-start | bytes 221192 | tf_op jit(solution)/shard_map/ppermute | solution.py:530
  38.5 4.4 %collective-permute-start.19 = (bf16[288,128]{1,0:T(8,128)(2,1)S(1)}, bf16[288,128]{1,0:T(8,128)(2,1)S(1)}, u32[]{:S(2)}, u32[]{:S(2)}) collective-permute-start(bf16[288,128]{1,0:T(8,128)(2,1)S(1)} %add_convert_fusion.refs_1_), channel_id=1, source_target_pairs={{0,4},{1,5},{2,6},{3,7},{4,0},{5,1},{6,2},{7,3},{8,12},{9,13},{10,... | collective-permute-start | bytes 221192 | tf_op jit(solution)/shard_map/ppermute | solution.py:530
  40.9 2.8 %collective-permute-start.17 = (bf16[288,128]{1,0:T(8,128)(2,1)S(1)}, bf16[288,128]{1,0:T(8,128)(2,1)S(1)}, u32[]{:S(2)}, u32[]{:S(2)}) collective-permute-start(bf16[288,128]{1,0:T(8,128)(2,1)S(1)} %collective-permute-done.15.refs_0_), channel_id=1, source_target_pairs={{0,1},{1,0},{2,3},{3,2},{4,5},{5,4},{6,7},{7,6},{8,9},{9,8},{10,11... | collective-permute-start | bytes 221192 | tf_op jit(solution)/shard_map/ppermute | solution.py:439
  42.4 1.3 %collective-permute-start.20 = (bf16[288,128]{1,0:T(8,128)(2,1)S(1)}, bf16[288,128]{1,0:T(8,128)(2,1)S(1)}, u32[]{:S(2)}, u32[]{:S(2)}) collective-permute-start(bf16[288,128]{1,0:T(8,128)(2,1)S(1)} %collective-permute-done.18.refs_1_), channel_id=1, source_target_pairs={{0,1},{1,0},{2,3},{3,2},{4,5},{5,4},{6,7},{7,6},{8,9},{9,8},{10,11... | collective-permute-start | bytes 221192 | tf_op jit(solution)/shard_map/ppermute | solution.py:439
  42.8 1.3 %collective-permute-start.21 = (bf16[288,128]{1,0:T(8,128)(2,1)S(1)}, bf16[288,128]{1,0:T(8,128)(2,1)S(1)}, u32[]{:S(2)}, u32[]{:S(2)}) collective-permute-start(bf16[288,128]{1,0:T(8,128)(2,1)S(1)} %collective-permute-done.19.refs_2_), channel_id=1, source_target_pairs={{0,1},{1,0},{2,3},{3,2},{4,5},{5,4},{6,7},{7,6},{8,9},{9,8},{10,11... | collective-permute-start | bytes 221192 | tf_op jit(solution)/shard_map/ppermute | solution.py:439
  (4 other events, 7.2 us)

commit v2 on v1

--- a/solution.py
+++ b/solution.py
@@ -266,16 +266,14 @@
         near = slots[slot][...].astype(F32)
         far = slots[slot + 2][...].astype(F32)
         for both, packed in ((sums, near + far), (diffs, sign * (near - far))):
-            rows = unpack(packed.astype(BF))
-            both[0, spot] = rows
-            both[1, spot] = swap_groups(rows)
-
-
-def to_modes(table, cells):
+            both[spot] = unpack(packed.astype(BF))
+
+
+def to_modes(table, cells, factor):
     size = table.shape[0] // 2
-    straight, crossed = (cells[i].reshape(-1, cells.shape[-1]) for i in range(2))
-    real = dot(table[:size], straight)
-    imag = dot(table[size:], crossed)
+    rows = cells[...].reshape(-1, cells.shape[-1])
+    real = (dot(table[:size], rows) * factor).astype(BF)
+    imag = swap_groups((dot(table[size:], rows) * factor).astype(BF))
     return choose(real, imag), choose(imag, real)
 
 
@@ -319,9 +317,9 @@
     sums, diffs = refs[10:]
     load_halves(lax.axis_index("lon"), slots, sums, diffs)
     for parity, half in ((0, sums), (1, diffs)):
-        modes = to_modes(fwd_ref[parity], half)
+        modes = to_modes(fwd_ref[parity], half, 1.0)
         for group in range(2):
-            spec = modes[group].astype(BF)
+            spec = modes[group]
             act, slope = gelu_both(dot(spec, first_ref[group]))
             act = act.astype(BF)
             size = act.shape[0]
@@ -358,12 +356,12 @@
     load_halves(lax.axis_index("lon"), slots, sums, diffs)
     terms = [[0.0, 0.0], [0.0, 0.0]]
     for parity, half in ((0, sums), (1, diffs)):
-        modes = to_modes(fwd_ref[parity], half)
-        factor = mode_factor(modes[0].shape, parity, lat_rows)
-        size = modes[0].shape[0]
+        size = fwd_ref.shape[1] // 2
+        factor = mode_factor((size, half.shape[-1]), parity, lat_rows)
+        modes = to_modes(fwd_ref[parity], half, factor)
         span = slice(parity * size, (parity + 1) * size)
         for group in range(2):
-            dual = (modes[group] * factor).astype(BF)
+            dual = modes[group]
             pre = (dot(dual, second_ref[group]) * slope_ref[parity, group]).astype(BF)
             pre_ref[parity, group] = pre
             terms[0][group] += dot(spec_t[group, :, span], pre)
@@ -475,7 +473,7 @@
     def own(weight):
         return lax.dynamic_slice_in_dim(weight, lax.axis_index("lon") * 2, 2, axis=1)
 
-    halves = [pltpu.VMEM((2, 2, rows, width), BF)] * 2
+    halves = [pltpu.VMEM((2, rows, width), BF)] * 2
     results = [pltpu.VMEM((2, rows, width), F32)] * 2
 
     field_slots = trade(call(pack_kernel, [packed] * 4, [fields]))
@@ -521,7 +519,7 @@
     while mask < sample_count:
         other = swap(grad, "dp", mask)
         if mask == 4:
-            other, layer_out, pull_slots[1:3] = after(other, layer_out, pull_slots[1:3])
+            other, layer_out, pull_slots[2] = after(other, layer_out, pull_slots[2])
         grad = added(grad, other)
         mask *= 2
     beside = swap(grad, "lon", 1)
@@ -550,10 +548,9 @@
     early = spread(((2, 1), (0, 0), (1, 0)), [corner, grad, beside])
     across, *early = after(across, *early)
     across_core, flipped_core = swap(across, "lon", 1), swap(flipped, "lon", 1)
+    early = spread(((2, 0), (3, 1)), [across, corner_core], early)
     first_grad, second_grad = spread(
-        ((3, 1), (2, 0), (0, 1), (3, 0), (1, 1)),
-        [corner_core, across, flipped, across_core, flipped_core],
-        early,
+        ((0, 1), (3, 0), (1, 1)), [flipped, across_core, flipped_core], early
     )
     return layer_out, field_grad, first_grad, second_grad
 

time: 45.6 us -> 45.4 us (level)
  waiting for transfers between devices: 7.67 us -> 5.11 us
  starting transfers between devices: 19.3 us -> 20.9 us
  Pallas kernels: 12.8 us -> 13.4 us
    ppermute x19, waiting for transfers between devices: 5.88 us -> 3.42 us  [swap(): return lax.ppermute(value, axis, [(i, i ^ mask) for i in range(size)])]
    ppermute x19, starting transfers between devices: 15.8 us -> 17.4 us  [swap(): return lax.ppermute(value, axis, [(i, i ^ mask) for i in range(size)])]
    pallas_call x11 -> x12, Pallas kernels: 12.8 us -> 13.4 us  [call(): pl.pallas_call(kernel, out_shape=outs, in_specs=[HBM if i in in_hbm or i...]
  transfers between devices with their start and end apart: 22 -> 22, of which waited for: 10 -> 7; matrix products, arithmetic and copies ran while one was open for 2% -> 2% of each run, Pallas kernels for 25% -> 27%
where the time goes in v2:
time: 45.4 us; the launch traced here: 45.1 us
  starting transfers between devices  20.9 us (46%)
  Pallas kernels  13.4 us (30%)
  waiting for transfers between devices  5.11 us (11%)
  local copies, waits for them, and re-layouts  4.75 us (10%)
  between operations  0.79 us (2%)
    ppermute x19, starting transfers between devices, swap(): return lax.ppermute(value, axis, [(i, i ^ mask) for i in range(size)])  17.4 us
    pallas_call x12, Pallas kernels, call(): pl.pallas_call(kernel, out_shape=outs, in_specs=[HBM if i in in_hbm or i...  13.4 us
    unnamed x12, local copies, waits for them, and re-layouts  3.8 us
    ppermute x3, starting transfers between devices, by_groups(): lax.ppermute(grad, ('dp', 'lon'), flip_pairs(sample_count, lon_count, d, i))  3.55 us
    ppermute x19, waiting for transfers between devices, swap(): return lax.ppermute(value, axis, [(i, i ^ mask) for i in range(size)])  3.42 us
    ppermute x3, waiting for transfers between devices, by_groups(): lax.ppermute(grad, ('dp', 'lon'), flip_pairs(sample_count, lon_count, d, i))  1.69 us
    dynamic_slice x1, local copies, waits for them, and re-layouts, own(): lax.dynamic_slice_in_dim(weight, lax.axis_index('lon') * 2, 2, axis=1)  0.96 us
  transfers between devices with their start and end apart: 22, of which 7 were waited for; matrix products, arithmetic and copies ran while one was open for 2% of the time, Pallas kernels for 27%

profile of v2, /device:TPU:0, one launch (start us, length us, event | category | flops | bytes accessed | tf_op | source)
XLA Modules:
  0.0 45.1 jit_solution(15445731644870460243)
XLA Ops:
  0.6 1.1 %copy-done.1 = bf16[1,8,48,768]{3,2,1,0:T(8,128)(2,1)S(1)} copy-done((bf16[1,8,48,768]{3,2,1,0:T(8,128)(2,1)S(1)}, bf16[1,8,48,768]{3,2,1,0:T(8,128)(2,1)}, u32[]{:S(2)}) %copy-start.1) | copy-done | bytes 589848
  2.5 2.6 %collective-permute-start.4 = (bf16[576,128]{1,0:T(8,128)(2,1)S(1)}, bf16[576,128]{1,0:T(8,128)(2,1)S(1)}, u32[]{:S(2)}, u32[]{:S(2)}) collective-permute-start(bf16[576,128]{1,0:T(8,128)(2,1)S(1)} %get-tuple-element.66), channel_id=1, source_target_pairs={{0,2},{1,3},{2,0},{3,1},{4,6},{5,7},{6,4},{7,5},{8,10},{9,11},{10,... | collective-permute-start | bytes 442376 | tf_op jit(solution)/shard_map/ppermute | solution.py:437
  5.2 1.1 %copy-done.3 = bf16[1,8,48,768]{3,2,1,0:T(8,128)(2,1)S(1)} copy-done((bf16[1,8,48,768]{3,2,1,0:T(8,128)(2,1)S(1)}, bf16[1,8,48,768]{3,2,1,0:T(8,128)(2,1)}, u32[]{:S(2)}) %copy-start.3) | copy-done | bytes 589848
  6.7 1.9 %collective-permute-start.1 = (bf16[576,128]{1,0:T(8,128)(2,1)S(1)}, bf16[576,128]{1,0:T(8,128)(2,1)S(1)}, u32[]{:S(2)}, u32[]{:S(2)}) collective-permute-start(bf16[576,128]{1,0:T(8,128)(2,1)S(1)} %get-tuple-element.62), channel_id=1, source_target_pairs={{0,2},{1,3},{2,0},{3,1},{4,6},{5,7},{6,4},{7,5},{8,10},{9,11},{10,... | collective-permute-start | bytes 442376 | tf_op jit(solution)/shard_map/ppermute | solution.py:437
  8.6 1.0 %constant_dynamic-slice_fusion = (bf16[2,2,96,96]{3,2,1,0:T(8,128)(2,1)S(1)}, bf16[2,2,96,96]{3,2,1,0:T(8,128)(2,1)S(1)}) fusion(bf16[2,8,96,96]{3,2,1,0:T(8,128)(2,1)} %param.9, s32[]{:T(128)S(6)} %select_n.4, bf16[2,8,96,96]{3,2,1,0:T(8,128)(2,1)} %param.8), kind=kLoop, calls=%fused_computation.3 | loop fusion | bytes 294916 | tf_op jit(solution)/shard_map/dynamic_slice | solution.py:474
  9.6 1.7 %copy-done.5 = bf16[2,768,768]{2,1,0:T(8,128)(2,1)S(1)} copy-done((bf16[2,768,768]{2,1,0:T(8,128)(2,1)S(1)}, bf16[2,768,768]{2,1,0:T(8,128)(2,1)}, u32[]{:S(2)}) %copy-start.5) | copy-done | bytes 2359320
  12.4 2.1 %shard_map.96 = (bf16[2,2,384,192]{3,2,1,0:T(8,128)(2,1)S(1)}, f32[2,2,384,192]{3,2,1,0:T(8,128)S(1)}, bf16[2,192,768]{2,1,0:T(8,128)(2,1)S(1)}, bf16[2,192,768]{2,1,0:T(8,128)(2,1)S(1)}) custom-call(bf16[576,128]{1,0:T(8,128)(2,1)S(1)} %get-tuple-element.64.refs_0_, bf16[576,128]{1,0:T(8,128)(2,1)S(1)} %collective-permute-done.3.refs_1_, ...), custom_call_target="tpu_custom_call" | custom-call | flops 1 | bytes 1 | tf_op jit(solution)/shard_map/pallas_call | solution.py:423
  14.6 1.4 %shard_map.97 = (bf16[576,128]{1,0:T(8,128)(2,1)S(1)}, bf16[576,128]{1,0:T(8,128)(2,1)S(1)}, bf16[576,128]{1,0:T(8,128)(2,1)S(1)}, bf16[576,128]{1,0:T(8,128)(2,1)S(1)}) custom-call(bf16[2,2,384,192]{3,2,1,0:T(8,128)(2,1)S(1)} %get-tuple-element.70.act_ref, bf16[2,768,768]{2,1,0:T(8,128)(2,1)S(1)} %copy-done, ...), custom_call_target="tpu_custom_call" | custom-call | flops 1 | bytes 1 | tf_op jit(solution)/shard_map/pallas_call | solution.py:423
  16.3 2.0 %collective-permute-start.8 = (bf16[576,128]{1,0:T(8,128)(2,1)S(1)}, bf16[576,128]{1,0:T(8,128)(2,1)S(1)}, u32[]{:S(2)}, u32[]{:S(2)}) collective-permute-start(bf16[576,128]{1,0:T(8,128)(2,1)S(1)} %get-tuple-element.74), channel_id=1, source_target_pairs={{0,2},{1,3},{2,0},{3,1},{4,6},{5,7},{6,4},{7,5},{8,10},{9,11},{10,... | collective-permute-start | bytes 442376 | tf_op jit(solution)/shard_map/ppermute | solution.py:437
  18.7 2.2 %shard_map.98 = (bf16[2,2,384,192]{3,2,1,0:T(8,128)(2,1)S(1)}, bf16[288,128]{1,0:T(8,128)(2,1)S(1)}, bf16[288,128]{1,0:T(8,128)(2,1)S(1)}) custom-call(bf16[576,128]{1,0:T(8,128)(2,1)S(1)} %get-tuple-element.76.refs_0_, bf16[576,128]{1,0:T(8,128)(2,1)S(1)} %collective-permute-done.refs_1_, bf16[576,128]{1,0:T(8,128)(2,1)S(1)} %collective-permute-done.1.refs_2_, ...), custom_call_target="tpu_custom_call" | custom-call | flops 1 | bytes 1 | tf_op jit(solution)/shard_map/pallas_call | solution.py:423
  20.9 1.6 %collective-permute-start.6 = (bf16[288,128]{1,0:T(8,128)(2,1)S(1)}, bf16[288,128]{1,0:T(8,128)(2,1)S(1)}, u32[]{:S(2)}, u32[]{:S(2)}) collective-permute-start(bf16[288,128]{1,0:T(8,128)(2,1)S(1)} %get-tuple-element.85), channel_id=1, source_target_pairs={{0,4},{4,0},{8,12},{12,8},{16,20},{20,16},{24,28},{28,24},{1,5},{5... | collective-permute-start | bytes 221192 | tf_op jit(solution)/shard_map/ppermute | solution.py:437
  22.5 1.3 %shard_map.99 = (bf16[576,128]{1,0:T(8,128)(2,1)S(1)}, bf16[576,128]{1,0:T(8,128)(2,1)S(1)}, bf16[576,128]{1,0:T(8,128)(2,1)S(1)}, bf16[576,128]{1,0:T(8,128)(2,1)S(1)}) custom-call(bf16[2,2,384,192]{3,2,1,0:T(8,128)(2,1)S(1)} %get-tuple-element.86.pre_ref, bf16[2,768,768]{2,1,0:T(8,128)(2,1)S(1)} %copy-done, ...), custom_call_target="tpu_custom_call" | custom-call | flops 1 | bytes 1 | tf_op jit(solution)/shard_map/pallas_call | solution.py:423
  23.9 1.5 %collective-permute-done.6 = bf16[288,128]{1,0:T(8,128)(2,1)S(1)} collective-permute-done((bf16[288,128]{1,0:T(8,128)(2,1)S(1)}, bf16[288,128]{1,0:T(8,128)(2,1)S(1)}, u32[]{:S(2)}, u32[]{:S(2)}) %collective-permute-start.6) | collective-permute-done | bytes 73760 | tf_op jit(solution)/shard_map/ppermute | solution.py:437
  25.4 1.8 %collective-permute-start.10 = (bf16[288,128]{1,0:T(8,128)(2,1)S(1)}, bf16[288,128]{1,0:T(8,128)(2,1)S(1)}, u32[]{:S(2)}, u32[]{:S(2)}) collective-permute-start(bf16[288,128]{1,0:T(8,128)(2,1)S(1)} %add_convert_fusion.2), channel_id=1, source_target_pairs={{0,8},{4,12},{8,0},{12,4},{16,24},{20,28},{24,16},{28,20},{1,9},{5... | collective-permute-start | bytes 221192 | tf_op jit(solution)/shard_map/ppermute | solution.py:437
  27.2 1.5 %collective-permute-start.12 = (bf16[576,128]{1,0:T(8,128)(2,1)S(1)}, bf16[576,128]{1,0:T(8,128)(2,1)S(1)}, u32[]{:S(2)}, u32[]{:S(2)}) collective-permute-start(bf16[576,128]{1,0:T(8,128)(2,1)S(1)} %get-tuple-element.97), channel_id=1, source_target_pairs={{0,2},{1,3},{2,0},{3,1},{4,6},{5,7},{6,4},{7,5},{8,10},{9,11},{10,... | collective-permute-start | bytes 442376 | tf_op jit(solution)/shard_map/ppermute | solution.py:437
  28.7 1.1 %collective-permute-done.10 = bf16[288,128]{1,0:T(8,128)(2,1)S(1)} collective-permute-done((bf16[288,128]{1,0:T(8,128)(2,1)S(1)}, bf16[288,128]{1,0:T(8,128)(2,1)S(1)}, u32[]{:S(2)}, u32[]{:S(2)}) %collective-permute-start.10) | collective-permute-done | bytes 73760 | tf_op jit(solution)/shard_map/ppermute | solution.py:437
  29.8 2.8 %collective-permute-start.11 = (bf16[288,128]{1,0:T(8,128)(2,1)S(1)}, bf16[288,128]{1,0:T(8,128)(2,1)S(1)}, u32[]{:S(2)}, u32[]{:S(2)}) collective-permute-start(bf16[288,128]{1,0:T(8,128)(2,1)S(1)} %add_convert_fusion.1), channel_id=1, source_target_pairs={{0,16},{4,20},{8,24},{12,28},{16,0},{20,4},{24,8},{28,12},{1,17},{... | collective-permute-start | bytes 221192 | tf_op jit(solution)/shard_map/ppermute | solution.py:437
  32.7 1.6 %collective-permute-start.16 = (bf16[576,128]{1,0:T(8,128)(2,1)S(1)}, bf16[576,128]{1,0:T(8,128)(2,1)S(1)}, u32[]{:S(2)}, u32[]{:S(2)}) collective-permute-start(bf16[576,128]{1,0:T(8,128)(2,1)S(1)} %get-tuple-element.103), channel_id=1, source_target_pairs={{0,3},{1,2},{2,1},{3,0},{4,7},{5,6},{6,5},{7,4},{8,11},{9,10},{10,... | collective-permute-start | bytes 442376 | tf_op jit(solution)/shard_map/ppermute | solution.py:437
  34.3 1.1 %shard_map.100 = bf16[1,8,48,768]{3,2,1,0:T(8,128)(2,1)} custom-call(bf16[1,8,48,768]{3,2,1,0:T(8,128)(2,1)S(1)} %copy-done.2, bf16[576,128]{1,0:T(8,128)(2,1)S(1)} %get-tuple-element.93.refs_0_, bf16[576,128]{1,0:T(8,128)(2,1)S(1)} %collective-permute-done.7.refs_1_, bf16[576,128]{1,0:T(8,128)(2,1)S(1)} %collective-permute-done.8.refs_2_, ...), custom_call_target="tpu_custom_call" | custom-call | flops 1 | bytes 1 | tf_op jit(solution)/shard_map/pallas_call | solution.py:423
  35.4 2.5 %collective-permute-start.14 = (bf16[288,128]{1,0:T(8,128)(2,1)S(1)}, bf16[288,128]{1,0:T(8,128)(2,1)S(1)}, u32[]{:S(2)}, u32[]{:S(2)}) collective-permute-start(bf16[288,128]{1,0:T(8,128)(2,1)S(1)} %add_convert_fusion.refs_1_), channel_id=1, source_target_pairs={{0,6},{1,7},{2,4},{3,5},{4,2},{5,3},{6,0},{7,1},{8,14},{9,15},{10,... | collective-permute-start | bytes 221192 | tf_op jit(solution)/shard_map/ppermute | solution.py:528
  39.0 1.1 %shard_map.101 = bf16[1,8,48,768]{3,2,1,0:T(8,128)(2,1)} custom-call(bf16[1,8,48,768]{3,2,1,0:T(8,128)(2,1)S(1)} %copy-done.4, bf16[576,128]{1,0:T(8,128)(2,1)S(1)} %get-tuple-element.100.refs_0_, bf16[576,128]{1,0:T(8,128)(2,1)S(1)} %collective-permute-done.15.refs_1_, bf16[576,128]{1,0:T(8,128)(2,1)S(1)} %collective-permute-done.12.refs_2_, ...), custom_call_target="tpu_custom_call" | custom-call | flops 1 | bytes 1 | tf_op jit(solution)/shard_map/pallas_call | solution.py:423
  40.1 1.0 %collective-permute-done.14.refs_0_ = bf16[288,128]{1,0:T(8,128)(2,1)S(1)} collective-permute-done((bf16[288,128]{1,0:T(8,128)(2,1)S(1)}, bf16[288,128]{1,0:T(8,128)(2,1)S(1)}, u32[]{:S(2)}, u32[]{:S(2)}) %collective-permute-start.14) | collective-permute-done | bytes 73760 | tf_op jit(solution)/shard_map/ppermute | solution.py:528
  41.1 1.0 %shard_map.102 = (f32[2,8,96,96]{3,2,1,0:T(8,128)}, f32[2,8,96,96]{3,2,1,0:T(8,128)}) custom-call(bf16[288,128]{1,0:T(8,128)(2,1)S(1)} %collective-permute-done.14.refs_0_, bf16[288,128]{1,0:T(8,128)(2,1)S(1)} %add_convert_fusion.refs_1_, bf16[288,128]{1,0:T(8,128)(2,1)S(1)} %collective-permute-done.13.refs_2_), custom_call_target="tpu_custom_call" | custom-call | flops 1 | bytes 1 | tf_op jit(solution)/shard_map/pallas_call | solution.py:423
  44.1 1.0 %shard_map.104 = (f32[2,8,96,96]{3,2,1,0:T(8,128)}, f32[2,8,96,96]{3,2,1,0:T(8,128)}) custom-call(bf16[288,128]{1,0:T(8,128)(2,1)S(1)} %collective-permute-done.17.refs_0_, bf16[288,128]{1,0:T(8,128)(2,1)S(1)} %collective-permute-done.19.refs_1_, bf16[288,128]{1,0:T(8,128)(2,1)S(1)} %collective-permute-done.20.refs_2_, ...), custom_call_target="tpu_custom_call", output_to_operand_aliasing={{0}: (3, {}), {1}: (4, {})} | custom-call | flops 1 | bytes 1 | tf_op jit(solution)/shard_map/pallas_call | solution.py:423
  (48 shorter events, 6.7 us)
Async XLA Ops:
  2.0 6.6 %collective-permute-start.3 = (bf16[576,128]{1,0:T(8,128)(2,1)S(1)}, bf16[576,128]{1,0:T(8,128)(2,1)S(1)}, u32[]{:S(2)}, u32[]{:S(2)}) collective-permute-start(bf16[576,128]{1,0:T(8,128)(2,1)S(1)} %get-tuple-element.65), channel_id=1, source_target_pairs={{0,1},{1,0},{2,3},{3,2},{4,5},{5,4},{6,7},{7,6},{8,9},{9,8},{10,11... | collective-permute-start | bytes 442376 | tf_op jit(solution)/shard_map/ppermute | solution.py:437
  2.5 9.5 %collective-permute-start.4 = (bf16[576,128]{1,0:T(8,128)(2,1)S(1)}, bf16[576,128]{1,0:T(8,128)(2,1)S(1)}, u32[]{:S(2)}, u32[]{:S(2)}) collective-permute-start(bf16[576,128]{1,0:T(8,128)(2,1)S(1)} %get-tuple-element.66), channel_id=1, source_target_pairs={{0,2},{1,3},{2,0},{3,1},{4,6},{5,7},{6,4},{7,5},{8,10},{9,11},{10,... | collective-permute-start | bytes 442376 | tf_op jit(solution)/shard_map/ppermute | solution.py:437
  5.1 7.3 %collective-permute-start.5 = (bf16[576,128]{1,0:T(8,128)(2,1)S(1)}, bf16[576,128]{1,0:T(8,128)(2,1)S(1)}, u32[]{:S(2)}, u32[]{:S(2)}) collective-permute-start(bf16[576,128]{1,0:T(8,128)(2,1)S(1)} %get-tuple-element.67), channel_id=1, source_target_pairs={{0,3},{1,2},{2,1},{3,0},{4,7},{5,6},{6,5},{7,4},{8,11},{9,10},{10,... | collective-permute-start | bytes 442376 | tf_op jit(solution)/shard_map/ppermute | solution.py:437
  6.5 11.8 %collective-permute-start = (bf16[576,128]{1,0:T(8,128)(2,1)S(1)}, bf16[576,128]{1,0:T(8,128)(2,1)S(1)}, u32[]{:S(2)}, u32[]{:S(2)}) collective-permute-start(bf16[576,128]{1,0:T(8,128)(2,1)S(1)} %get-tuple-element.61), channel_id=1, source_target_pairs={{0,1},{1,0},{2,3},{3,2},{4,5},{5,4},{6,7},{7,6},{8,9},{9,8},{10,11... | collective-permute-start | bytes 442376 | tf_op jit(solution)/shard_map/ppermute | solution.py:437
  6.7 11.6 %collective-permute-start.1 = (bf16[576,128]{1,0:T(8,128)(2,1)S(1)}, bf16[576,128]{1,0:T(8,128)(2,1)S(1)}, u32[]{:S(2)}, u32[]{:S(2)}) collective-permute-start(bf16[576,128]{1,0:T(8,128)(2,1)S(1)} %get-tuple-element.62), channel_id=1, source_target_pairs={{0,2},{1,3},{2,0},{3,1},{4,6},{5,7},{6,4},{7,5},{8,10},{9,11},{10,... | collective-permute-start | bytes 442376 | tf_op jit(solution)/shard_map/ppermute | solution.py:437
  8.6 10.1 %collective-permute-start.2 = (bf16[576,128]{1,0:T(8,128)(2,1)S(1)}, bf16[576,128]{1,0:T(8,128)(2,1)S(1)}, u32[]{:S(2)}, u32[]{:S(2)}) collective-permute-start(bf16[576,128]{1,0:T(8,128)(2,1)S(1)} %get-tuple-element.63), channel_id=1, source_target_pairs={{0,3},{1,2},{2,1},{3,0},{4,7},{5,6},{6,5},{7,4},{8,11},{9,10},{10,... | collective-permute-start | bytes 442376 | tf_op jit(solution)/shard_map/ppermute | solution.py:437
  15.9 9.4 %collective-permute-start.7 = (bf16[576,128]{1,0:T(8,128)(2,1)S(1)}, bf16[576,128]{1,0:T(8,128)(2,1)S(1)}, u32[]{:S(2)}, u32[]{:S(2)}) collective-permute-start(bf16[576,128]{1,0:T(8,128)(2,1)S(1)} %get-tuple-element.73), channel_id=1, source_target_pairs={{0,1},{1,0},{2,3},{3,2},{4,5},{5,4},{6,7},{7,6},{8,9},{9,8},{10,11... | collective-permute-start | bytes 442376 | tf_op jit(solution)/shard_map/ppermute | solution.py:437
  16.3 9.0 %collective-permute-start.8 = (bf16[576,128]{1,0:T(8,128)(2,1)S(1)}, bf16[576,128]{1,0:T(8,128)(2,1)S(1)}, u32[]{:S(2)}, u32[]{:S(2)}) collective-permute-start(bf16[576,128]{1,0:T(8,128)(2,1)S(1)} %get-tuple-element.74), channel_id=1, source_target_pairs={{0,2},{1,3},{2,0},{3,1},{4,6},{5,7},{6,4},{7,5},{8,10},{9,11},{10,... | collective-permute-start | bytes 442376 | tf_op jit(solution)/shard_map/ppermute | solution.py:437
  18.3 7.1 %collective-permute-start.9 = (bf16[576,128]{1,0:T(8,128)(2,1)S(1)}, bf16[576,128]{1,0:T(8,128)(2,1)S(1)}, u32[]{:S(2)}, u32[]{:S(2)}) collective-permute-start(bf16[576,128]{1,0:T(8,128)(2,1)S(1)} %get-tuple-element.75), channel_id=1, source_target_pairs={{0,3},{1,2},{2,1},{3,0},{4,7},{5,6},{6,5},{7,4},{8,11},{9,10},{10,... | collective-permute-start | bytes 442376 | tf_op jit(solution)/shard_map/ppermute | solution.py:437
  20.9 13.4 %copy-start.2 = (bf16[1,8,48,768]{3,2,1,0:T(8,128)(2,1)S(1)}, bf16[1,8,48,768]{3,2,1,0:T(8,128)(2,1)}, u32[]{:S(2)}) copy-start(bf16[1,8,48,768]{3,2,1,0:T(8,128)(2,1)} %grid_ref.6) | copy-start | bytes 1769476
  20.9 4.4 %collective-permute-start.6 = (bf16[288,128]{1,0:T(8,128)(2,1)S(1)}, bf16[288,128]{1,0:T(8,128)(2,1)S(1)}, u32[]{:S(2)}, u32[]{:S(2)}) collective-permute-start(bf16[288,128]{1,0:T(8,128)(2,1)S(1)} %get-tuple-element.85), channel_id=1, source_target_pairs={{0,4},{4,0},{8,12},{12,8},{16,20},{20,16},{24,28},{28,24},{1,5},{5... | collective-permute-start | bytes 221192 | tf_op jit(solution)/shard_map/ppermute | solution.py:437
  22.5 16.5 %copy-start.4 = (bf16[1,8,48,768]{3,2,1,0:T(8,128)(2,1)S(1)}, bf16[1,8,48,768]{3,2,1,0:T(8,128)(2,1)}, u32[]{:S(2)}) copy-start(bf16[1,8,48,768]{3,2,1,0:T(8,128)(2,1)} %grid_ref.7) | copy-start | bytes 1769476
  25.4 4.4 %collective-permute-start.10 = (bf16[288,128]{1,0:T(8,128)(2,1)S(1)}, bf16[288,128]{1,0:T(8,128)(2,1)S(1)}, u32[]{:S(2)}, u32[]{:S(2)}) collective-permute-start(bf16[288,128]{1,0:T(8,128)(2,1)S(1)} %add_convert_fusion.2), channel_id=1, source_target_pairs={{0,8},{4,12},{8,0},{12,4},{16,24},{20,28},{24,16},{28,20},{1,9},{5... | collective-permute-start | bytes 221192 | tf_op jit(solution)/shard_map/ppermute | solution.py:437
  27.2 8.1 %collective-permute-start.12 = (bf16[576,128]{1,0:T(8,128)(2,1)S(1)}, bf16[576,128]{1,0:T(8,128)(2,1)S(1)}, u32[]{:S(2)}, u32[]{:S(2)}) collective-permute-start(bf16[576,128]{1,0:T(8,128)(2,1)S(1)} %get-tuple-element.97), channel_id=1, source_target_pairs={{0,2},{1,3},{2,0},{3,1},{4,6},{5,7},{6,4},{7,5},{8,10},{9,11},{10,... | collective-permute-start | bytes 442376 | tf_op jit(solution)/shard_map/ppermute | solution.py:437
  29.8 5.5 %collective-permute-start.11 = (bf16[288,128]{1,0:T(8,128)(2,1)S(1)}, bf16[288,128]{1,0:T(8,128)(2,1)S(1)}, u32[]{:S(2)}, u32[]{:S(2)}) collective-permute-start(bf16[288,128]{1,0:T(8,128)(2,1)S(1)} %add_convert_fusion.1), channel_id=1, source_target_pairs={{0,16},{4,20},{8,24},{12,28},{16,0},{20,4},{24,8},{28,12},{1,17},{... | collective-permute-start | bytes 221192 | tf_op jit(solution)/shard_map/ppermute | solution.py:437
  32.7 5.8 %collective-permute-start.15 = (bf16[576,128]{1,0:T(8,128)(2,1)S(1)}, bf16[576,128]{1,0:T(8,128)(2,1)S(1)}, u32[]{:S(2)}, u32[]{:S(2)}) collective-permute-start(bf16[576,128]{1,0:T(8,128)(2,1)S(1)} %get-tuple-element.101), channel_id=1, source_target_pairs={{0,1},{1,0},{2,3},{3,2},{4,5},{5,4},{6,7},{7,6},{8,9},{9,8},{10,11... | collective-permute-start | bytes 442376 | tf_op jit(solution)/shard_map/ppermute | solution.py:437
  32.7 6.3 %collective-permute-start.16 = (bf16[576,128]{1,0:T(8,128)(2,1)S(1)}, bf16[576,128]{1,0:T(8,128)(2,1)S(1)}, u32[]{:S(2)}, u32[]{:S(2)}) collective-permute-start(bf16[576,128]{1,0:T(8,128)(2,1)S(1)} %get-tuple-element.103), channel_id=1, source_target_pairs={{0,3},{1,2},{2,1},{3,0},{4,7},{5,6},{6,5},{7,4},{8,11},{9,10},{10,... | collective-permute-start | bytes 442376 | tf_op jit(solution)/shard_map/ppermute | solution.py:437
  35.4 4.7 %collective-permute-start.13 = (bf16[288,128]{1,0:T(8,128)(2,1)S(1)}, bf16[288,128]{1,0:T(8,128)(2,1)S(1)}, u32[]{:S(2)}, u32[]{:S(2)}) collective-permute-start(bf16[288,128]{1,0:T(8,128)(2,1)S(1)} %add_convert_fusion.refs_1_), channel_id=1, source_target_pairs={{0,1},{1,0},{2,3},{3,2},{4,5},{5,4},{6,7},{7,6},{8,9},{9,8},{10,11... | collective-permute-start | bytes 221192 | tf_op jit(solution)/shard_map/ppermute | solution.py:437
  35.4 5.6 %collective-permute-start.14 = (bf16[288,128]{1,0:T(8,128)(2,1)S(1)}, bf16[288,128]{1,0:T(8,128)(2,1)S(1)}, u32[]{:S(2)}, u32[]{:S(2)}) collective-permute-start(bf16[288,128]{1,0:T(8,128)(2,1)S(1)} %add_convert_fusion.refs_1_), channel_id=1, source_target_pairs={{0,6},{1,7},{2,4},{3,5},{4,2},{5,3},{6,0},{7,1},{8,14},{9,15},{10,... | collective-permute-start | bytes 221192 | tf_op jit(solution)/shard_map/ppermute | solution.py:528
  37.9 4.7 %collective-permute-start.18 = (bf16[288,128]{1,0:T(8,128)(2,1)S(1)}, bf16[288,128]{1,0:T(8,128)(2,1)S(1)}, u32[]{:S(2)}, u32[]{:S(2)}) collective-permute-start(bf16[288,128]{1,0:T(8,128)(2,1)S(1)} %add_convert_fusion.refs_1_), channel_id=1, source_target_pairs={{0,2},{1,3},{2,0},{3,1},{4,6},{5,7},{6,4},{7,5},{8,10},{9,11},{10,... | collective-permute-start | bytes 221192 | tf_op jit(solution)/shard_map/ppermute | solution.py:528
  38.5 4.4 %collective-permute-start.17 = (bf16[288,128]{1,0:T(8,128)(2,1)S(1)}, bf16[288,128]{1,0:T(8,128)(2,1)S(1)}, u32[]{:S(2)}, u32[]{:S(2)}) collective-permute-start(bf16[288,128]{1,0:T(8,128)(2,1)S(1)} %add_convert_fusion.refs_1_), channel_id=1, source_target_pairs={{0,4},{1,5},{2,6},{3,7},{4,0},{5,1},{6,2},{7,3},{8,12},{9,13},{10,... | collective-permute-start | bytes 221192 | tf_op jit(solution)/shard_map/ppermute | solution.py:528
  41.1 2.1 %collective-permute-start.21 = (bf16[288,128]{1,0:T(8,128)(2,1)S(1)}, bf16[288,128]{1,0:T(8,128)(2,1)S(1)}, u32[]{:S(2)}, u32[]{:S(2)}) collective-permute-start(bf16[288,128]{1,0:T(8,128)(2,1)S(1)} %collective-permute-done.14.refs_0_), channel_id=1, source_target_pairs={{0,1},{1,0},{2,3},{3,2},{4,5},{5,4},{6,7},{7,6},{8,9},{9,8},{10,11... | collective-permute-start | bytes 221192 | tf_op jit(solution)/shard_map/ppermute | solution.py:437
  42.6 1.4 %collective-permute-start.19 = (bf16[288,128]{1,0:T(8,128)(2,1)S(1)}, bf16[288,128]{1,0:T(8,128)(2,1)S(1)}, u32[]{:S(2)}, u32[]{:S(2)}) collective-permute-start(bf16[288,128]{1,0:T(8,128)(2,1)S(1)} %collective-permute-done.18.refs_0_), channel_id=1, source_target_pairs={{0,1},{1,0},{2,3},{3,2},{4,5},{5,4},{6,7},{7,6},{8,9},{9,8},{10,11... | collective-permute-start | bytes 221192 | tf_op jit(solution)/shard_map/ppermute | solution.py:437
  42.8 1.3 %collective-permute-start.20 = (bf16[288,128]{1,0:T(8,128)(2,1)S(1)}, bf16[288,128]{1,0:T(8,128)(2,1)S(1)}, u32[]{:S(2)}, u32[]{:S(2)}) collective-permute-start(bf16[288,128]{1,0:T(8,128)(2,1)S(1)} %collective-permute-done.17.refs_0_), channel_id=1, source_target_pairs={{0,1},{1,0},{2,3},{3,2},{4,5},{5,4},{6,7},{7,6},{8,9},{9,8},{10,11... | collective-permute-start | bytes 221192 | tf_op jit(solution)/shard_map/ppermute | solution.py:437
  (4 other events, 7.1 us)

commit v3 on v2

--- a/solution.py
+++ b/solution.py
@@ -548,9 +548,9 @@
     early = spread(((2, 1), (0, 0), (1, 0)), [corner, grad, beside])
     across, *early = after(across, *early)
     across_core, flipped_core = swap(across, "lon", 1), swap(flipped, "lon", 1)
-    early = spread(((2, 0), (3, 1)), [across, corner_core], early)
+    early = spread(((2, 0), (3, 1), (0, 1)), [across, corner_core, flipped], early)
     first_grad, second_grad = spread(
-        ((0, 1), (3, 0), (1, 1)), [flipped, across_core, flipped_core], early
+        ((3, 0), (1, 1)), [across_core, flipped_core], early
     )
     return layer_out, field_grad, first_grad, second_grad
 

time: 45.4 us -> 45.4 us (level)
  no operation moved by 1% of the time
where the time goes in v3:
time: 45.4 us; the launch traced here: 45.1 us
  starting transfers between devices  20.9 us (46%)
  Pallas kernels  13.4 us (30%)
  waiting for transfers between devices  5.09 us (11%)
  local copies, waits for them, and re-layouts  4.75 us (10%)
  between operations  0.79 us (2%)
    ppermute x19, starting transfers between devices, swap(): return lax.ppermute(value, axis, [(i, i ^ mask) for i in range(size)])  17.4 us
    pallas_call x12, Pallas kernels, call(): pl.pallas_call(kernel, out_shape=outs, in_specs=[HBM if i in in_hbm or i...  13.4 us
    unnamed x12, local copies, waits for them, and re-layouts  3.8 us
    ppermute x3, starting transfers between devices, by_groups(): lax.ppermute(grad, ('dp', 'lon'), flip_pairs(sample_count, lon_count, d, i))  3.55 us
    ppermute x19, waiting for transfers between devices, swap(): return lax.ppermute(value, axis, [(i, i ^ mask) for i in range(size)])  3.4 us
    ppermute x3, waiting for transfers between devices, by_groups(): lax.ppermute(grad, ('dp', 'lon'), flip_pairs(sample_count, lon_count, d, i))  1.69 us
    dynamic_slice x1, local copies, waits for them, and re-layouts, own(): lax.dynamic_slice_in_dim(weight, lax.axis_index('lon') * 2, 2, axis=1)  0.96 us
  transfers between devices with their start and end apart: 22, of which 7 were waited for; matrix products, arithmetic and copies ran while one was open for 2% of the time, Pallas kernels for 27%

profile of v3, /device:TPU:0, one launch (start us, length us, event | category | flops | bytes accessed | tf_op | source)
XLA Modules:
  0.0 45.1 jit_solution(16733566979693385826)
XLA Ops:
  0.6 1.1 %copy-done.1 = bf16[1,8,48,768]{3,2,1,0:T(8,128)(2,1)S(1)} copy-done((bf16[1,8,48,768]{3,2,1,0:T(8,128)(2,1)S(1)}, bf16[1,8,48,768]{3,2,1,0:T(8,128)(2,1)}, u32[]{:S(2)}) %copy-start.1) | copy-done | bytes 589848
  2.5 2.6 %collective-permute-start.4 = (bf16[576,128]{1,0:T(8,128)(2,1)S(1)}, bf16[576,128]{1,0:T(8,128)(2,1)S(1)}, u32[]{:S(2)}, u32[]{:S(2)}) collective-permute-start(bf16[576,128]{1,0:T(8,128)(2,1)S(1)} %get-tuple-element.66), channel_id=1, source_target_pairs={{0,2},{1,3},{2,0},{3,1},{4,6},{5,7},{6,4},{7,5},{8,10},{9,11},{10,... | collective-permute-start | bytes 442376 | tf_op jit(solution)/shard_map/ppermute | solution.py:437
  5.2 1.1 %copy-done.3 = bf16[1,8,48,768]{3,2,1,0:T(8,128)(2,1)S(1)} copy-done((bf16[1,8,48,768]{3,2,1,0:T(8,128)(2,1)S(1)}, bf16[1,8,48,768]{3,2,1,0:T(8,128)(2,1)}, u32[]{:S(2)}) %copy-start.3) | copy-done | bytes 589848
  6.7 1.9 %collective-permute-start.1 = (bf16[576,128]{1,0:T(8,128)(2,1)S(1)}, bf16[576,128]{1,0:T(8,128)(2,1)S(1)}, u32[]{:S(2)}, u32[]{:S(2)}) collective-permute-start(bf16[576,128]{1,0:T(8,128)(2,1)S(1)} %get-tuple-element.62), channel_id=1, source_target_pairs={{0,2},{1,3},{2,0},{3,1},{4,6},{5,7},{6,4},{7,5},{8,10},{9,11},{10,... | collective-permute-start | bytes 442376 | tf_op jit(solution)/shard_map/ppermute | solution.py:437
  8.6 1.0 %constant_dynamic-slice_fusion = (bf16[2,2,96,96]{3,2,1,0:T(8,128)(2,1)S(1)}, bf16[2,2,96,96]{3,2,1,0:T(8,128)(2,1)S(1)}) fusion(bf16[2,8,96,96]{3,2,1,0:T(8,128)(2,1)} %param.9, s32[]{:T(128)S(6)} %select_n.4, bf16[2,8,96,96]{3,2,1,0:T(8,128)(2,1)} %param.8), kind=kLoop, calls=%fused_computation.3 | loop fusion | bytes 294916 | tf_op jit(solution)/shard_map/dynamic_slice | solution.py:474
  9.6 1.7 %copy-done.5 = bf16[2,768,768]{2,1,0:T(8,128)(2,1)S(1)} copy-done((bf16[2,768,768]{2,1,0:T(8,128)(2,1)S(1)}, bf16[2,768,768]{2,1,0:T(8,128)(2,1)}, u32[]{:S(2)}) %copy-start.5) | copy-done | bytes 2359320
  12.4 2.1 %shard_map.96 = (bf16[2,2,384,192]{3,2,1,0:T(8,128)(2,1)S(1)}, f32[2,2,384,192]{3,2,1,0:T(8,128)S(1)}, bf16[2,192,768]{2,1,0:T(8,128)(2,1)S(1)}, bf16[2,192,768]{2,1,0:T(8,128)(2,1)S(1)}) custom-call(bf16[576,128]{1,0:T(8,128)(2,1)S(1)} %get-tuple-element.64.refs_0_, bf16[576,128]{1,0:T(8,128)(2,1)S(1)} %collective-permute-done.3.refs_1_, ...), custom_call_target="tpu_custom_call" | custom-call | flops 1 | bytes 1 | tf_op jit(solution)/shard_map/pallas_call | solution.py:423
  14.6 1.4 %shard_map.97 = (bf16[576,128]{1,0:T(8,128)(2,1)S(1)}, bf16[576,128]{1,0:T(8,128)(2,1)S(1)}, bf16[576,128]{1,0:T(8,128)(2,1)S(1)}, bf16[576,128]{1,0:T(8,128)(2,1)S(1)}) custom-call(bf16[2,2,384,192]{3,2,1,0:T(8,128)(2,1)S(1)} %get-tuple-element.70.act_ref, bf16[2,768,768]{2,1,0:T(8,128)(2,1)S(1)} %copy-done, ...), custom_call_target="tpu_custom_call" | custom-call | flops 1 | bytes 1 | tf_op jit(solution)/shard_map/pallas_call | solution.py:423
  16.3 2.0 %collective-permute-start.8 = (bf16[576,128]{1,0:T(8,128)(2,1)S(1)}, bf16[576,128]{1,0:T(8,128)(2,1)S(1)}, u32[]{:S(2)}, u32[]{:S(2)}) collective-permute-start(bf16[576,128]{1,0:T(8,128)(2,1)S(1)} %get-tuple-element.74), channel_id=1, source_target_pairs={{0,2},{1,3},{2,0},{3,1},{4,6},{5,7},{6,4},{7,5},{8,10},{9,11},{10,... | collective-permute-start | bytes 442376 | tf_op jit(solution)/shard_map/ppermute | solution.py:437
  18.7 2.2 %shard_map.98 = (bf16[2,2,384,192]{3,2,1,0:T(8,128)(2,1)S(1)}, bf16[288,128]{1,0:T(8,128)(2,1)S(1)}, bf16[288,128]{1,0:T(8,128)(2,1)S(1)}) custom-call(bf16[576,128]{1,0:T(8,128)(2,1)S(1)} %get-tuple-element.76.refs_0_, bf16[576,128]{1,0:T(8,128)(2,1)S(1)} %collective-permute-done.refs_1_, bf16[576,128]{1,0:T(8,128)(2,1)S(1)} %collective-permute-done.1.refs_2_, ...), custom_call_target="tpu_custom_call" | custom-call | flops 1 | bytes 1 | tf_op jit(solution)/shard_map/pallas_call | solution.py:423
  20.9 1.6 %collective-permute-start.6 = (bf16[288,128]{1,0:T(8,128)(2,1)S(1)}, bf16[288,128]{1,0:T(8,128)(2,1)S(1)}, u32[]{:S(2)}, u32[]{:S(2)}) collective-permute-start(bf16[288,128]{1,0:T(8,128)(2,1)S(1)} %get-tuple-element.85), channel_id=1, source_target_pairs={{0,4},{4,0},{8,12},{12,8},{16,20},{20,16},{24,28},{28,24},{1,5},{5... | collective-permute-start | bytes 221192 | tf_op jit(solution)/shard_map/ppermute | solution.py:437
  22.5 1.3 %shard_map.99 = (bf16[576,128]{1,0:T(8,128)(2,1)S(1)}, bf16[576,128]{1,0:T(8,128)(2,1)S(1)}, bf16[576,128]{1,0:T(8,128)(2,1)S(1)}, bf16[576,128]{1,0:T(8,128)(2,1)S(1)}) custom-call(bf16[2,2,384,192]{3,2,1,0:T(8,128)(2,1)S(1)} %get-tuple-element.86.pre_ref, bf16[2,768,768]{2,1,0:T(8,128)(2,1)S(1)} %copy-done, ...), custom_call_target="tpu_custom_call" | custom-call | flops 1 | bytes 1 | tf_op jit(solution)/shard_map/pallas_call | solution.py:423
  23.9 1.5 %collective-permute-done.6 = bf16[288,128]{1,0:T(8,128)(2,1)S(1)} collective-permute-done((bf16[288,128]{1,0:T(8,128)(2,1)S(1)}, bf16[288,128]{1,0:T(8,128)(2,1)S(1)}, u32[]{:S(2)}, u32[]{:S(2)}) %collective-permute-start.6) | collective-permute-done | bytes 73760 | tf_op jit(solution)/shard_map/ppermute | solution.py:437
  25.4 1.8 %collective-permute-start.10 = (bf16[288,128]{1,0:T(8,128)(2,1)S(1)}, bf16[288,128]{1,0:T(8,128)(2,1)S(1)}, u32[]{:S(2)}, u32[]{:S(2)}) collective-permute-start(bf16[288,128]{1,0:T(8,128)(2,1)S(1)} %add_convert_fusion.2), channel_id=1, source_target_pairs={{0,8},{4,12},{8,0},{12,4},{16,24},{20,28},{24,16},{28,20},{1,9},{5... | collective-permute-start | bytes 221192 | tf_op jit(solution)/shard_map/ppermute | solution.py:437
  27.2 1.5 %collective-permute-start.12 = (bf16[576,128]{1,0:T(8,128)(2,1)S(1)}, bf16[576,128]{1,0:T(8,128)(2,1)S(1)}, u32[]{:S(2)}, u32[]{:S(2)}) collective-permute-start(bf16[576,128]{1,0:T(8,128)(2,1)S(1)} %get-tuple-element.97), channel_id=1, source_target_pairs={{0,2},{1,3},{2,0},{3,1},{4,6},{5,7},{6,4},{7,5},{8,10},{9,11},{10,... | collective-permute-start | bytes 442376 | tf_op jit(solution)/shard_map/ppermute | solution.py:437
  28.7 1.1 %collective-permute-done.10 = bf16[288,128]{1,0:T(8,128)(2,1)S(1)} collective-permute-done((bf16[288,128]{1,0:T(8,128)(2,1)S(1)}, bf16[288,128]{1,0:T(8,128)(2,1)S(1)}, u32[]{:S(2)}, u32[]{:S(2)}) %collective-permute-start.10) | collective-permute-done | bytes 73760 | tf_op jit(solution)/shard_map/ppermute | solution.py:437
  29.8 2.8 %collective-permute-start.11 = (bf16[288,128]{1,0:T(8,128)(2,1)S(1)}, bf16[288,128]{1,0:T(8,128)(2,1)S(1)}, u32[]{:S(2)}, u32[]{:S(2)}) collective-permute-start(bf16[288,128]{1,0:T(8,128)(2,1)S(1)} %add_convert_fusion.1), channel_id=1, source_target_pairs={{0,16},{4,20},{8,24},{12,28},{16,0},{20,4},{24,8},{28,12},{1,17},{... | collective-permute-start | bytes 221192 | tf_op jit(solution)/shard_map/ppermute | solution.py:437
  32.7 1.6 %collective-permute-start.16 = (bf16[576,128]{1,0:T(8,128)(2,1)S(1)}, bf16[576,128]{1,0:T(8,128)(2,1)S(1)}, u32[]{:S(2)}, u32[]{:S(2)}) collective-permute-start(bf16[576,128]{1,0:T(8,128)(2,1)S(1)} %get-tuple-element.103), channel_id=1, source_target_pairs={{0,3},{1,2},{2,1},{3,0},{4,7},{5,6},{6,5},{7,4},{8,11},{9,10},{10,... | collective-permute-start | bytes 442376 | tf_op jit(solution)/shard_map/ppermute | solution.py:437
  34.3 1.1 %shard_map.100 = bf16[1,8,48,768]{3,2,1,0:T(8,128)(2,1)} custom-call(bf16[1,8,48,768]{3,2,1,0:T(8,128)(2,1)S(1)} %copy-done.2, bf16[576,128]{1,0:T(8,128)(2,1)S(1)} %get-tuple-element.93.refs_0_, bf16[576,128]{1,0:T(8,128)(2,1)S(1)} %collective-permute-done.7.refs_1_, bf16[576,128]{1,0:T(8,128)(2,1)S(1)} %collective-permute-done.8.refs_2_, ...), custom_call_target="tpu_custom_call" | custom-call | flops 1 | bytes 1 | tf_op jit(solution)/shard_map/pallas_call | solution.py:423
  35.4 2.5 %collective-permute-start.14 = (bf16[288,128]{1,0:T(8,128)(2,1)S(1)}, bf16[288,128]{1,0:T(8,128)(2,1)S(1)}, u32[]{:S(2)}, u32[]{:S(2)}) collective-permute-start(bf16[288,128]{1,0:T(8,128)(2,1)S(1)} %add_convert_fusion.refs_1_), channel_id=1, source_target_pairs={{0,6},{1,7},{2,4},{3,5},{4,2},{5,3},{6,0},{7,1},{8,14},{9,15},{10,... | collective-permute-start | bytes 221192 | tf_op jit(solution)/shard_map/ppermute | solution.py:528
  39.0 1.1 %shard_map.101 = bf16[1,8,48,768]{3,2,1,0:T(8,128)(2,1)} custom-call(bf16[1,8,48,768]{3,2,1,0:T(8,128)(2,1)S(1)} %copy-done.4, bf16[576,128]{1,0:T(8,128)(2,1)S(1)} %get-tuple-element.100.refs_0_, bf16[576,128]{1,0:T(8,128)(2,1)S(1)} %collective-permute-done.15.refs_1_, bf16[576,128]{1,0:T(8,128)(2,1)S(1)} %collective-permute-done.12.refs_2_, ...), custom_call_target="tpu_custom_call" | custom-call | flops 1 | bytes 1 | tf_op jit(solution)/shard_map/pallas_call | solution.py:423
  40.1 1.0 %collective-permute-done.14.refs_0_ = bf16[288,128]{1,0:T(8,128)(2,1)S(1)} collective-permute-done((bf16[288,128]{1,0:T(8,128)(2,1)S(1)}, bf16[288,128]{1,0:T(8,128)(2,1)S(1)}, u32[]{:S(2)}, u32[]{:S(2)}) %collective-permute-start.14) | collective-permute-done | bytes 73760 | tf_op jit(solution)/shard_map/ppermute | solution.py:528
  41.1 1.0 %shard_map.102 = (f32[2,8,96,96]{3,2,1,0:T(8,128)}, f32[2,8,96,96]{3,2,1,0:T(8,128)}) custom-call(bf16[288,128]{1,0:T(8,128)(2,1)S(1)} %collective-permute-done.14.refs_0_, bf16[288,128]{1,0:T(8,128)(2,1)S(1)} %add_convert_fusion.refs_1_, bf16[288,128]{1,0:T(8,128)(2,1)S(1)} %collective-permute-done.13.refs_2_), custom_call_target="tpu_custom_call" | custom-call | flops 1 | bytes 1 | tf_op jit(solution)/shard_map/pallas_call | solution.py:423
  43.1 1.0 %shard_map.103 = (f32[2,8,96,96]{3,2,1,0:T(8,128)}, f32[2,8,96,96]{3,2,1,0:T(8,128)}) custom-call(bf16[288,128]{1,0:T(8,128)(2,1)S(1)} %collective-permute-done.17.refs_0_, bf16[288,128]{1,0:T(8,128)(2,1)S(1)} %collective-permute-done.21.refs_1_, bf16[288,128]{1,0:T(8,128)(2,1)S(1)} %collective-permute-done.19.refs_2_, ...), custom_call_target="tpu_custom_call", output_to_operand_aliasing={{0}: (3, {}), {1}: (4, {})} | custom-call | flops 1 | bytes 1 | tf_op jit(solution)/shard_map/pallas_call | solution.py:423
  (48 shorter events, 6.7 us)
Async XLA Ops:
  2.0 6.6 %collective-permute-start.3 = (bf16[576,128]{1,0:T(8,128)(2,1)S(1)}, bf16[576,128]{1,0:T(8,128)(2,1)S(1)}, u32[]{:S(2)}, u32[]{:S(2)}) collective-permute-start(bf16[576,128]{1,0:T(8,128)(2,1)S(1)} %get-tuple-element.65), channel_id=1, source_target_pairs={{0,1},{1,0},{2,3},{3,2},{4,5},{5,4},{6,7},{7,6},{8,9},{9,8},{10,11... | collective-permute-start | bytes 442376 | tf_op jit(solution)/shard_map/ppermute | solution.py:437
  2.5 9.5 %collective-permute-start.4 = (bf16[576,128]{1,0:T(8,128)(2,1)S(1)}, bf16[576,128]{1,0:T(8,128)(2,1)S(1)}, u32[]{:S(2)}, u32[]{:S(2)}) collective-permute-start(bf16[576,128]{1,0:T(8,128)(2,1)S(1)} %get-tuple-element.66), channel_id=1, source_target_pairs={{0,2},{1,3},{2,0},{3,1},{4,6},{5,7},{6,4},{7,5},{8,10},{9,11},{10,... | collective-permute-start | bytes 442376 | tf_op jit(solution)/shard_map/ppermute | solution.py:437
  5.1 7.3 %collective-permute-start.5 = (bf16[576,128]{1,0:T(8,128)(2,1)S(1)}, bf16[576,128]{1,0:T(8,128)(2,1)S(1)}, u32[]{:S(2)}, u32[]{:S(2)}) collective-permute-start(bf16[576,128]{1,0:T(8,128)(2,1)S(1)} %get-tuple-element.67), channel_id=1, source_target_pairs={{0,3},{1,2},{2,1},{3,0},{4,7},{5,6},{6,5},{7,4},{8,11},{9,10},{10,... | collective-permute-start | bytes 442376 | tf_op jit(solution)/shard_map/ppermute | solution.py:437
  6.5 11.8 %collective-permute-start = (bf16[576,128]{1,0:T(8,128)(2,1)S(1)}, bf16[576,128]{1,0:T(8,128)(2,1)S(1)}, u32[]{:S(2)}, u32[]{:S(2)}) collective-permute-start(bf16[576,128]{1,0:T(8,128)(2,1)S(1)} %get-tuple-element.61), channel_id=1, source_target_pairs={{0,1},{1,0},{2,3},{3,2},{4,5},{5,4},{6,7},{7,6},{8,9},{9,8},{10,11... | collective-permute-start | bytes 442376 | tf_op jit(solution)/shard_map/ppermute | solution.py:437
  6.7 11.6 %collective-permute-start.1 = (bf16[576,128]{1,0:T(8,128)(2,1)S(1)}, bf16[576,128]{1,0:T(8,128)(2,1)S(1)}, u32[]{:S(2)}, u32[]{:S(2)}) collective-permute-start(bf16[576,128]{1,0:T(8,128)(2,1)S(1)} %get-tuple-element.62), channel_id=1, source_target_pairs={{0,2},{1,3},{2,0},{3,1},{4,6},{5,7},{6,4},{7,5},{8,10},{9,11},{10,... | collective-permute-start | bytes 442376 | tf_op jit(solution)/shard_map/ppermute | solution.py:437
  8.6 10.1 %collective-permute-start.2 = (bf16[576,128]{1,0:T(8,128)(2,1)S(1)}, bf16[576,128]{1,0:T(8,128)(2,1)S(1)}, u32[]{:S(2)}, u32[]{:S(2)}) collective-permute-start(bf16[576,128]{1,0:T(8,128)(2,1)S(1)} %get-tuple-element.63), channel_id=1, source_target_pairs={{0,3},{1,2},{2,1},{3,0},{4,7},{5,6},{6,5},{7,4},{8,11},{9,10},{10,... | collective-permute-start | bytes 442376 | tf_op jit(solution)/shard_map/ppermute | solution.py:437
  15.9 9.4 %collective-permute-start.7 = (bf16[576,128]{1,0:T(8,128)(2,1)S(1)}, bf16[576,128]{1,0:T(8,128)(2,1)S(1)}, u32[]{:S(2)}, u32[]{:S(2)}) collective-permute-start(bf16[576,128]{1,0:T(8,128)(2,1)S(1)} %get-tuple-element.73), channel_id=1, source_target_pairs={{0,1},{1,0},{2,3},{3,2},{4,5},{5,4},{6,7},{7,6},{8,9},{9,8},{10,11... | collective-permute-start | bytes 442376 | tf_op jit(solution)/shard_map/ppermute | solution.py:437
  16.3 9.0 %collective-permute-start.8 = (bf16[576,128]{1,0:T(8,128)(2,1)S(1)}, bf16[576,128]{1,0:T(8,128)(2,1)S(1)}, u32[]{:S(2)}, u32[]{:S(2)}) collective-permute-start(bf16[576,128]{1,0:T(8,128)(2,1)S(1)} %get-tuple-element.74), channel_id=1, source_target_pairs={{0,2},{1,3},{2,0},{3,1},{4,6},{5,7},{6,4},{7,5},{8,10},{9,11},{10,... | collective-permute-start | bytes 442376 | tf_op jit(solution)/shard_map/ppermute | solution.py:437
  18.3 7.1 %collective-permute-start.9 = (bf16[576,128]{1,0:T(8,128)(2,1)S(1)}, bf16[576,128]{1,0:T(8,128)(2,1)S(1)}, u32[]{:S(2)}, u32[]{:S(2)}) collective-permute-start(bf16[576,128]{1,0:T(8,128)(2,1)S(1)} %get-tuple-element.75), channel_id=1, source_target_pairs={{0,3},{1,2},{2,1},{3,0},{4,7},{5,6},{6,5},{7,4},{8,11},{9,10},{10,... | collective-permute-start | bytes 442376 | tf_op jit(solution)/shard_map/ppermute | solution.py:437
  20.9 13.4 %copy-start.2 = (bf16[1,8,48,768]{3,2,1,0:T(8,128)(2,1)S(1)}, bf16[1,8,48,768]{3,2,1,0:T(8,128)(2,1)}, u32[]{:S(2)}) copy-start(bf16[1,8,48,768]{3,2,1,0:T(8,128)(2,1)} %grid_ref.6) | copy-start | bytes 1769476
  20.9 4.4 %collective-permute-start.6 = (bf16[288,128]{1,0:T(8,128)(2,1)S(1)}, bf16[288,128]{1,0:T(8,128)(2,1)S(1)}, u32[]{:S(2)}, u32[]{:S(2)}) collective-permute-start(bf16[288,128]{1,0:T(8,128)(2,1)S(1)} %get-tuple-element.85), channel_id=1, source_target_pairs={{0,4},{4,0},{8,12},{12,8},{16,20},{20,16},{24,28},{28,24},{1,5},{5... | collective-permute-start | bytes 221192 | tf_op jit(solution)/shard_map/ppermute | solution.py:437
  22.5 16.5 %copy-start.4 = (bf16[1,8,48,768]{3,2,1,0:T(8,128)(2,1)S(1)}, bf16[1,8,48,768]{3,2,1,0:T(8,128)(2,1)}, u32[]{:S(2)}) copy-start(bf16[1,8,48,768]{3,2,1,0:T(8,128)(2,1)} %grid_ref.7) | copy-start | bytes 1769476
  25.4 4.4 %collective-permute-start.10 = (bf16[288,128]{1,0:T(8,128)(2,1)S(1)}, bf16[288,128]{1,0:T(8,128)(2,1)S(1)}, u32[]{:S(2)}, u32[]{:S(2)}) collective-permute-start(bf16[288,128]{1,0:T(8,128)(2,1)S(1)} %add_convert_fusion.2), channel_id=1, source_target_pairs={{0,8},{4,12},{8,0},{12,4},{16,24},{20,28},{24,16},{28,20},{1,9},{5... | collective-permute-start | bytes 221192 | tf_op jit(solution)/shard_map/ppermute | solution.py:437
  27.2 8.1 %collective-permute-start.12 = (bf16[576,128]{1,0:T(8,128)(2,1)S(1)}, bf16[576,128]{1,0:T(8,128)(2,1)S(1)}, u32[]{:S(2)}, u32[]{:S(2)}) collective-permute-start(bf16[576,128]{1,0:T(8,128)(2,1)S(1)} %get-tuple-element.97), channel_id=1, source_target_pairs={{0,2},{1,3},{2,0},{3,1},{4,6},{5,7},{6,4},{7,5},{8,10},{9,11},{10,... | collective-permute-start | bytes 442376 | tf_op jit(solution)/shard_map/ppermute | solution.py:437
  29.8 5.5 %collective-permute-start.11 = (bf16[288,128]{1,0:T(8,128)(2,1)S(1)}, bf16[288,128]{1,0:T(8,128)(2,1)S(1)}, u32[]{:S(2)}, u32[]{:S(2)}) collective-permute-start(bf16[288,128]{1,0:T(8,128)(2,1)S(1)} %add_convert_fusion.1), channel_id=1, source_target_pairs={{0,16},{4,20},{8,24},{12,28},{16,0},{20,4},{24,8},{28,12},{1,17},{... | collective-permute-start | bytes 221192 | tf_op jit(solution)/shard_map/ppermute | solution.py:437
  32.7 5.8 %collective-permute-start.15 = (bf16[576,128]{1,0:T(8,128)(2,1)S(1)}, bf16[576,128]{1,0:T(8,128)(2,1)S(1)}, u32[]{:S(2)}, u32[]{:S(2)}) collective-permute-start(bf16[576,128]{1,0:T(8,128)(2,1)S(1)} %get-tuple-element.101), channel_id=1, source_target_pairs={{0,1},{1,0},{2,3},{3,2},{4,5},{5,4},{6,7},{7,6},{8,9},{9,8},{10,11... | collective-permute-start | bytes 442376 | tf_op jit(solution)/shard_map/ppermute | solution.py:437
  32.7 6.3 %collective-permute-start.16 = (bf16[576,128]{1,0:T(8,128)(2,1)S(1)}, bf16[576,128]{1,0:T(8,128)(2,1)S(1)}, u32[]{:S(2)}, u32[]{:S(2)}) collective-permute-start(bf16[576,128]{1,0:T(8,128)(2,1)S(1)} %get-tuple-element.103), channel_id=1, source_target_pairs={{0,3},{1,2},{2,1},{3,0},{4,7},{5,6},{6,5},{7,4},{8,11},{9,10},{10,... | collective-permute-start | bytes 442376 | tf_op jit(solution)/shard_map/ppermute | solution.py:437
  35.4 4.7 %collective-permute-start.13 = (bf16[288,128]{1,0:T(8,128)(2,1)S(1)}, bf16[288,128]{1,0:T(8,128)(2,1)S(1)}, u32[]{:S(2)}, u32[]{:S(2)}) collective-permute-start(bf16[288,128]{1,0:T(8,128)(2,1)S(1)} %add_convert_fusion.refs_1_), channel_id=1, source_target_pairs={{0,1},{1,0},{2,3},{3,2},{4,5},{5,4},{6,7},{7,6},{8,9},{9,8},{10,11... | collective-permute-start | bytes 221192 | tf_op jit(solution)/shard_map/ppermute | solution.py:437
  35.4 5.6 %collective-permute-start.14 = (bf16[288,128]{1,0:T(8,128)(2,1)S(1)}, bf16[288,128]{1,0:T(8,128)(2,1)S(1)}, u32[]{:S(2)}, u32[]{:S(2)}) collective-permute-start(bf16[288,128]{1,0:T(8,128)(2,1)S(1)} %add_convert_fusion.refs_1_), channel_id=1, source_target_pairs={{0,6},{1,7},{2,4},{3,5},{4,2},{5,3},{6,0},{7,1},{8,14},{9,15},{10,... | collective-permute-start | bytes 221192 | tf_op jit(solution)/shard_map/ppermute | solution.py:528
  37.9 4.7 %collective-permute-start.17 = (bf16[288,128]{1,0:T(8,128)(2,1)S(1)}, bf16[288,128]{1,0:T(8,128)(2,1)S(1)}, u32[]{:S(2)}, u32[]{:S(2)}) collective-permute-start(bf16[288,128]{1,0:T(8,128)(2,1)S(1)} %add_convert_fusion.refs_1_), channel_id=1, source_target_pairs={{0,2},{1,3},{2,0},{3,1},{4,6},{5,7},{6,4},{7,5},{8,10},{9,11},{10,... | collective-permute-start | bytes 221192 | tf_op jit(solution)/shard_map/ppermute | solution.py:528
  38.5 4.4 %collective-permute-start.19 = (bf16[288,128]{1,0:T(8,128)(2,1)S(1)}, bf16[288,128]{1,0:T(8,128)(2,1)S(1)}, u32[]{:S(2)}, u32[]{:S(2)}) collective-permute-start(bf16[288,128]{1,0:T(8,128)(2,1)S(1)} %add_convert_fusion.refs_1_), channel_id=1, source_target_pairs={{0,4},{1,5},{2,6},{3,7},{4,0},{5,1},{6,2},{7,3},{8,12},{9,13},{10,... | collective-permute-start | bytes 221192 | tf_op jit(solution)/shard_map/ppermute | solution.py:528
  41.1 2.1 %collective-permute-start.21 = (bf16[288,128]{1,0:T(8,128)(2,1)S(1)}, bf16[288,128]{1,0:T(8,128)(2,1)S(1)}, u32[]{:S(2)}, u32[]{:S(2)}) collective-permute-start(bf16[288,128]{1,0:T(8,128)(2,1)S(1)} %collective-permute-done.14.refs_0_), channel_id=1, source_target_pairs={{0,1},{1,0},{2,3},{3,2},{4,5},{5,4},{6,7},{7,6},{8,9},{9,8},{10,11... | collective-permute-start | bytes 221192 | tf_op jit(solution)/shard_map/ppermute | solution.py:437
  42.6 1.5 %collective-permute-start.18 = (bf16[288,128]{1,0:T(8,128)(2,1)S(1)}, bf16[288,128]{1,0:T(8,128)(2,1)S(1)}, u32[]{:S(2)}, u32[]{:S(2)}) collective-permute-start(bf16[288,128]{1,0:T(8,128)(2,1)S(1)} %collective-permute-done.17.refs_0_), channel_id=1, source_target_pairs={{0,1},{1,0},{2,3},{3,2},{4,5},{5,4},{6,7},{7,6},{8,9},{9,8},{10,11... | collective-permute-start | bytes 221192 | tf_op jit(solution)/shard_map/ppermute | solution.py:437
  42.8 1.3 %collective-permute-start.20 = (bf16[288,128]{1,0:T(8,128)(2,1)S(1)}, bf16[288,128]{1,0:T(8,128)(2,1)S(1)}, u32[]{:S(2)}, u32[]{:S(2)}) collective-permute-start(bf16[288,128]{1,0:T(8,128)(2,1)S(1)} %collective-permute-done.19.refs_2_), channel_id=1, source_target_pairs={{0,1},{1,0},{2,3},{3,2},{4,5},{5,4},{6,7},{7,6},{8,9},{9,8},{10,11... | collective-permute-start | bytes 221192 | tf_op jit(solution)/shard_map/ppermute | solution.py:437
  (4 other events, 7.1 us)

commit v4 on v3

--- a/solution.py
+++ b/solution.py
@@ -324,7 +324,7 @@
             act = act.astype(BF)
             size = act.shape[0]
             act_ref[parity, group] = act
-            slope_ref[parity, group] = slope
+            slope_ref[parity, group] = slope.astype(BF)
             spec_t[group, :, parity * size : (parity + 1) * size] = spec.T
             act_t[group, :, parity * size : (parity + 1) * size] = act.T
 
@@ -362,7 +362,7 @@
         span = slice(parity * size, (parity + 1) * size)
         for group in range(2):
             dual = modes[group]
-            pre = (dot(dual, second_ref[group]) * slope_ref[parity, group]).astype(BF)
+            pre = (dot(dual, second_ref[group]) * slope_ref[parity, group].astype(F32)).astype(BF)
             pre_ref[parity, group] = pre
             terms[0][group] += dot(spec_t[group, :, span], pre)
             terms[1][group] += dot(act_t[group, :, span], dual)
@@ -489,7 +489,7 @@
         vmem_mib=48,
     )
     modes_shape = jax.ShapeDtypeStruct((2, 2, rows, width), BF)
-    slope_shape = jax.ShapeDtypeStruct((2, 2, rows, width), F32)
+    slope_shape = jax.ShapeDtypeStruct((2, 2, rows, width), BF)
     turned_shape = jax.ShapeDtypeStruct((2, width, half), BF)
     act, slope, spec_t, act_t = call(
         inner_kernel,

time: 45.4 us -> 45.4 us (level)
  no operation moved by 1% of the time
where the time goes in v4:
time: 45.4 us; the launch traced here: 45.1 us
  starting transfers between devices  21 us (46%)
  Pallas kernels  13.5 us (30%)
  waiting for transfers between devices  5.06 us (11%)
  local copies, waits for them, and re-layouts  4.75 us (10%)
  between operations  0.79 us (2%)
    ppermute x19, starting transfers between devices, swap(): return lax.ppermute(value, axis, [(i, i ^ mask) for i in range(size)])  17.4 us
    pallas_call x12, Pallas kernels, call(): pl.pallas_call(kernel, out_shape=outs, in_specs=[HBM if i in in_hbm or i...  13.5 us
    unnamed x12, local copies, waits for them, and re-layouts  3.8 us
    ppermute x3, starting transfers between devices, by_groups(): lax.ppermute(grad, ('dp', 'lon'), flip_pairs(sample_count, lon_count, d, i))  3.55 us
    ppermute x19, waiting for transfers between devices, swap(): return lax.ppermute(value, axis, [(i, i ^ mask) for i in range(size)])  3.37 us
    ppermute x3, waiting for transfers between devices, by_groups(): lax.ppermute(grad, ('dp', 'lon'), flip_pairs(sample_count, lon_count, d, i))  1.69 us
    dynamic_slice x1, local copies, waits for them, and re-layouts, own(): lax.dynamic_slice_in_dim(weight, lax.axis_index('lon') * 2, 2, axis=1)  0.96 us
  transfers between devices with their start and end apart: 22, of which 7 were waited for; matrix products, arithmetic and copies ran while one was open for 2% of the time, Pallas kernels for 27%

profile of v4, /device:TPU:0, one launch (start us, length us, event | category | flops | bytes accessed | tf_op | source)
XLA Modules:
  0.0 45.1 jit_solution(3559596117922930767)
XLA Ops:
  0.6 1.1 %copy-done.1 = bf16[1,8,48,768]{3,2,1,0:T(8,128)(2,1)S(1)} copy-done((bf16[1,8,48,768]{3,2,1,0:T(8,128)(2,1)S(1)}, bf16[1,8,48,768]{3,2,1,0:T(8,128)(2,1)}, u32[]{:S(2)}) %copy-start.1) | copy-done | bytes 589848
  2.5 2.6 %collective-permute-start.4 = (bf16[576,128]{1,0:T(8,128)(2,1)S(1)}, bf16[576,128]{1,0:T(8,128)(2,1)S(1)}, u32[]{:S(2)}, u32[]{:S(2)}) collective-permute-start(bf16[576,128]{1,0:T(8,128)(2,1)S(1)} %get-tuple-element.66), channel_id=1, source_target_pairs={{0,2},{1,3},{2,0},{3,1},{4,6},{5,7},{6,4},{7,5},{8,10},{9,11},{10,... | collective-permute-start | bytes 442376 | tf_op jit(solution)/shard_map/ppermute | solution.py:437
  5.2 1.1 %copy-done.3 = bf16[1,8,48,768]{3,2,1,0:T(8,128)(2,1)S(1)} copy-done((bf16[1,8,48,768]{3,2,1,0:T(8,128)(2,1)S(1)}, bf16[1,8,48,768]{3,2,1,0:T(8,128)(2,1)}, u32[]{:S(2)}) %copy-start.3) | copy-done | bytes 589848
  6.7 1.9 %collective-permute-start.1 = (bf16[576,128]{1,0:T(8,128)(2,1)S(1)}, bf16[576,128]{1,0:T(8,128)(2,1)S(1)}, u32[]{:S(2)}, u32[]{:S(2)}) collective-permute-start(bf16[576,128]{1,0:T(8,128)(2,1)S(1)} %get-tuple-element.62), channel_id=1, source_target_pairs={{0,2},{1,3},{2,0},{3,1},{4,6},{5,7},{6,4},{7,5},{8,10},{9,11},{10,... | collective-permute-start | bytes 442376 | tf_op jit(solution)/shard_map/ppermute | solution.py:437
  8.6 1.0 %constant_dynamic-slice_fusion = (bf16[2,2,96,96]{3,2,1,0:T(8,128)(2,1)S(1)}, bf16[2,2,96,96]{3,2,1,0:T(8,128)(2,1)S(1)}) fusion(bf16[2,8,96,96]{3,2,1,0:T(8,128)(2,1)} %param.9, s32[]{:T(128)S(6)} %select_n.4, bf16[2,8,96,96]{3,2,1,0:T(8,128)(2,1)} %param.8), kind=kLoop, calls=%fused_computation.3 | loop fusion | bytes 294916 | tf_op jit(solution)/shard_map/dynamic_slice | solution.py:474
  9.6 1.7 %copy-done.5 = bf16[2,768,768]{2,1,0:T(8,128)(2,1)S(1)} copy-done((bf16[2,768,768]{2,1,0:T(8,128)(2,1)S(1)}, bf16[2,768,768]{2,1,0:T(8,128)(2,1)}, u32[]{:S(2)}) %copy-start.5) | copy-done | bytes 2359320
  12.4 2.1 %shard_map.96 = (bf16[2,2,384,192]{3,2,1,0:T(8,128)(2,1)S(1)}, bf16[2,2,384,192]{3,2,1,0:T(8,128)(2,1)S(1)}, bf16[2,192,768]{2,1,0:T(8,128)(2,1)S(1)}, bf16[2,192,768]{2,1,0:T(8,128)(2,1)S(1)}) custom-call(bf16[576,128]{1,0:T(8,128)(2,1)S(1)} %get-tuple-element.64.refs_0_, bf16[576,128]{1,0:T(8,128)(2,1)S(1)} %collective-permute-done.3.refs_1_, ...), custom_call_target="tpu_custom_call" | custom-call | flops 1 | bytes 1 | tf_op jit(solution)/shard_map/pallas_call | solution.py:423
  14.6 1.4 %shard_map.97 = (bf16[576,128]{1,0:T(8,128)(2,1)S(1)}, bf16[576,128]{1,0:T(8,128)(2,1)S(1)}, bf16[576,128]{1,0:T(8,128)(2,1)S(1)}, bf16[576,128]{1,0:T(8,128)(2,1)S(1)}) custom-call(bf16[2,2,384,192]{3,2,1,0:T(8,128)(2,1)S(1)} %get-tuple-element.70.act_ref, bf16[2,768,768]{2,1,0:T(8,128)(2,1)S(1)} %copy-done, ...), custom_call_target="tpu_custom_call" | custom-call | flops 1 | bytes 1 | tf_op jit(solution)/shard_map/pallas_call | solution.py:423
  16.3 1.9 %collective-permute-start.8 = (bf16[576,128]{1,0:T(8,128)(2,1)S(1)}, bf16[576,128]{1,0:T(8,128)(2,1)S(1)}, u32[]{:S(2)}, u32[]{:S(2)}) collective-permute-start(bf16[576,128]{1,0:T(8,128)(2,1)S(1)} %get-tuple-element.74), channel_id=1, source_target_pairs={{0,2},{1,3},{2,0},{3,1},{4,6},{5,7},{6,4},{7,5},{8,10},{9,11},{10,... | collective-permute-start | bytes 442376 | tf_op jit(solution)/shard_map/ppermute | solution.py:437
  18.7 2.2 %shard_map.98 = (bf16[2,2,384,192]{3,2,1,0:T(8,128)(2,1)S(1)}, bf16[288,128]{1,0:T(8,128)(2,1)S(1)}, bf16[288,128]{1,0:T(8,128)(2,1)S(1)}) custom-call(bf16[576,128]{1,0:T(8,128)(2,1)S(1)} %get-tuple-element.76.refs_0_, bf16[576,128]{1,0:T(8,128)(2,1)S(1)} %collective-permute-done.refs_1_, bf16[576,128]{1,0:T(8,128)(2,1)S(1)} %collective-permute-done.1.refs_2_, ...), custom_call_target="tpu_custom_call" | custom-call | flops 1 | bytes 1 | tf_op jit(solution)/shard_map/pallas_call | solution.py:423
  20.9 1.6 %collective-permute-start.6 = (bf16[288,128]{1,0:T(8,128)(2,1)S(1)}, bf16[288,128]{1,0:T(8,128)(2,1)S(1)}, u32[]{:S(2)}, u32[]{:S(2)}) collective-permute-start(bf16[288,128]{1,0:T(8,128)(2,1)S(1)} %get-tuple-element.85), channel_id=1, source_target_pairs={{0,4},{4,0},{8,12},{12,8},{16,20},{20,16},{24,28},{28,24},{1,5},{5... | collective-permute-start | bytes 221192 | tf_op jit(solution)/shard_map/ppermute | solution.py:437
  22.6 1.3 %shard_map.99 = (bf16[576,128]{1,0:T(8,128)(2,1)S(1)}, bf16[576,128]{1,0:T(8,128)(2,1)S(1)}, bf16[576,128]{1,0:T(8,128)(2,1)S(1)}, bf16[576,128]{1,0:T(8,128)(2,1)S(1)}) custom-call(bf16[2,2,384,192]{3,2,1,0:T(8,128)(2,1)S(1)} %get-tuple-element.86.pre_ref, bf16[2,768,768]{2,1,0:T(8,128)(2,1)S(1)} %copy-done, ...), custom_call_target="tpu_custom_call" | custom-call | flops 1 | bytes 1 | tf_op jit(solution)/shard_map/pallas_call | solution.py:423
  23.9 1.5 %collective-permute-done.6 = bf16[288,128]{1,0:T(8,128)(2,1)S(1)} collective-permute-done((bf16[288,128]{1,0:T(8,128)(2,1)S(1)}, bf16[288,128]{1,0:T(8,128)(2,1)S(1)}, u32[]{:S(2)}, u32[]{:S(2)}) %collective-permute-start.6) | collective-permute-done | bytes 73760 | tf_op jit(solution)/shard_map/ppermute | solution.py:437
  25.4 1.8 %collective-permute-start.10 = (bf16[288,128]{1,0:T(8,128)(2,1)S(1)}, bf16[288,128]{1,0:T(8,128)(2,1)S(1)}, u32[]{:S(2)}, u32[]{:S(2)}) collective-permute-start(bf16[288,128]{1,0:T(8,128)(2,1)S(1)} %add_convert_fusion.2), channel_id=1, source_target_pairs={{0,8},{4,12},{8,0},{12,4},{16,24},{20,28},{24,16},{28,20},{1,9},{5... | collective-permute-start | bytes 221192 | tf_op jit(solution)/shard_map/ppermute | solution.py:437
  27.2 1.5 %collective-permute-start.12 = (bf16[576,128]{1,0:T(8,128)(2,1)S(1)}, bf16[576,128]{1,0:T(8,128)(2,1)S(1)}, u32[]{:S(2)}, u32[]{:S(2)}) collective-permute-start(bf16[576,128]{1,0:T(8,128)(2,1)S(1)} %get-tuple-element.97), channel_id=1, source_target_pairs={{0,2},{1,3},{2,0},{3,1},{4,6},{5,7},{6,4},{7,5},{8,10},{9,11},{10,... | collective-permute-start | bytes 442376 | tf_op jit(solution)/shard_map/ppermute | solution.py:437
  28.7 1.1 %collective-permute-done.10 = bf16[288,128]{1,0:T(8,128)(2,1)S(1)} collective-permute-done((bf16[288,128]{1,0:T(8,128)(2,1)S(1)}, bf16[288,128]{1,0:T(8,128)(2,1)S(1)}, u32[]{:S(2)}, u32[]{:S(2)}) %collective-permute-start.10) | collective-permute-done | bytes 73760 | tf_op jit(solution)/shard_map/ppermute | solution.py:437
  29.8 2.8 %collective-permute-start.11 = (bf16[288,128]{1,0:T(8,128)(2,1)S(1)}, bf16[288,128]{1,0:T(8,128)(2,1)S(1)}, u32[]{:S(2)}, u32[]{:S(2)}) collective-permute-start(bf16[288,128]{1,0:T(8,128)(2,1)S(1)} %add_convert_fusion.1), channel_id=1, source_target_pairs={{0,16},{4,20},{8,24},{12,28},{16,0},{20,4},{24,8},{28,12},{1,17},{... | collective-permute-start | bytes 221192 | tf_op jit(solution)/shard_map/ppermute | solution.py:437
  32.7 1.6 %collective-permute-start.16 = (bf16[576,128]{1,0:T(8,128)(2,1)S(1)}, bf16[576,128]{1,0:T(8,128)(2,1)S(1)}, u32[]{:S(2)}, u32[]{:S(2)}) collective-permute-start(bf16[576,128]{1,0:T(8,128)(2,1)S(1)} %get-tuple-element.103), channel_id=1, source_target_pairs={{0,3},{1,2},{2,1},{3,0},{4,7},{5,6},{6,5},{7,4},{8,11},{9,10},{10,... | collective-permute-start | bytes 442376 | tf_op jit(solution)/shard_map/ppermute | solution.py:437
  34.3 1.1 %shard_map.100 = bf16[1,8,48,768]{3,2,1,0:T(8,128)(2,1)} custom-call(bf16[1,8,48,768]{3,2,1,0:T(8,128)(2,1)S(1)} %copy-done.2, bf16[576,128]{1,0:T(8,128)(2,1)S(1)} %get-tuple-element.93.refs_0_, bf16[576,128]{1,0:T(8,128)(2,1)S(1)} %collective-permute-done.7.refs_1_, bf16[576,128]{1,0:T(8,128)(2,1)S(1)} %collective-permute-done.8.refs_2_, ...), custom_call_target="tpu_custom_call" | custom-call | flops 1 | bytes 1 | tf_op jit(solution)/shard_map/pallas_call | solution.py:423
  35.5 2.5 %collective-permute-start.14 = (bf16[288,128]{1,0:T(8,128)(2,1)S(1)}, bf16[288,128]{1,0:T(8,128)(2,1)S(1)}, u32[]{:S(2)}, u32[]{:S(2)}) collective-permute-start(bf16[288,128]{1,0:T(8,128)(2,1)S(1)} %add_convert_fusion.refs_1_), channel_id=1, source_target_pairs={{0,6},{1,7},{2,4},{3,5},{4,2},{5,3},{6,0},{7,1},{8,14},{9,15},{10,... | collective-permute-start | bytes 221192 | tf_op jit(solution)/shard_map/ppermute | solution.py:528
  39.0 1.1 %shard_map.101 = bf16[1,8,48,768]{3,2,1,0:T(8,128)(2,1)} custom-call(bf16[1,8,48,768]{3,2,1,0:T(8,128)(2,1)S(1)} %copy-done.4, bf16[576,128]{1,0:T(8,128)(2,1)S(1)} %get-tuple-element.100.refs_0_, bf16[576,128]{1,0:T(8,128)(2,1)S(1)} %collective-permute-done.15.refs_1_, bf16[576,128]{1,0:T(8,128)(2,1)S(1)} %collective-permute-done.12.refs_2_, ...), custom_call_target="tpu_custom_call" | custom-call | flops 1 | bytes 1 | tf_op jit(solution)/shard_map/pallas_call | solution.py:423
  40.1 1.0 %collective-permute-done.14.refs_0_ = bf16[288,128]{1,0:T(8,128)(2,1)S(1)} collective-permute-done((bf16[288,128]{1,0:T(8,128)(2,1)S(1)}, bf16[288,128]{1,0:T(8,128)(2,1)S(1)}, u32[]{:S(2)}, u32[]{:S(2)}) %collective-permute-start.14) | collective-permute-done | bytes 73760 | tf_op jit(solution)/shard_map/ppermute | solution.py:528
  41.1 1.0 %shard_map.102 = (f32[2,8,96,96]{3,2,1,0:T(8,128)}, f32[2,8,96,96]{3,2,1,0:T(8,128)}) custom-call(bf16[288,128]{1,0:T(8,128)(2,1)S(1)} %collective-permute-done.14.refs_0_, bf16[288,128]{1,0:T(8,128)(2,1)S(1)} %add_convert_fusion.refs_1_, bf16[288,128]{1,0:T(8,128)(2,1)S(1)} %collective-permute-done.13.refs_2_), custom_call_target="tpu_custom_call" | custom-call | flops 1 | bytes 1 | tf_op jit(solution)/shard_map/pallas_call | solution.py:423
  43.1 1.0 %shard_map.103 = (f32[2,8,96,96]{3,2,1,0:T(8,128)}, f32[2,8,96,96]{3,2,1,0:T(8,128)}) custom-call(bf16[288,128]{1,0:T(8,128)(2,1)S(1)} %collective-permute-done.17.refs_0_, bf16[288,128]{1,0:T(8,128)(2,1)S(1)} %collective-permute-done.21.refs_1_, bf16[288,128]{1,0:T(8,128)(2,1)S(1)} %collective-permute-done.19.refs_2_, ...), custom_call_target="tpu_custom_call", output_to_operand_aliasing={{0}: (3, {}), {1}: (4, {})} | custom-call | flops 1 | bytes 1 | tf_op jit(solution)/shard_map/pallas_call | solution.py:423
  (48 shorter events, 6.7 us)
Async XLA Ops:
  2.0 6.6 %collective-permute-start.3 = (bf16[576,128]{1,0:T(8,128)(2,1)S(1)}, bf16[576,128]{1,0:T(8,128)(2,1)S(1)}, u32[]{:S(2)}, u32[]{:S(2)}) collective-permute-start(bf16[576,128]{1,0:T(8,128)(2,1)S(1)} %get-tuple-element.65), channel_id=1, source_target_pairs={{0,1},{1,0},{2,3},{3,2},{4,5},{5,4},{6,7},{7,6},{8,9},{9,8},{10,11... | collective-permute-start | bytes 442376 | tf_op jit(solution)/shard_map/ppermute | solution.py:437
  2.5 9.5 %collective-permute-start.4 = (bf16[576,128]{1,0:T(8,128)(2,1)S(1)}, bf16[576,128]{1,0:T(8,128)(2,1)S(1)}, u32[]{:S(2)}, u32[]{:S(2)}) collective-permute-start(bf16[576,128]{1,0:T(8,128)(2,1)S(1)} %get-tuple-element.66), channel_id=1, source_target_pairs={{0,2},{1,3},{2,0},{3,1},{4,6},{5,7},{6,4},{7,5},{8,10},{9,11},{10,... | collective-permute-start | bytes 442376 | tf_op jit(solution)/shard_map/ppermute | solution.py:437
  5.1 7.3 %collective-permute-start.5 = (bf16[576,128]{1,0:T(8,128)(2,1)S(1)}, bf16[576,128]{1,0:T(8,128)(2,1)S(1)}, u32[]{:S(2)}, u32[]{:S(2)}) collective-permute-start(bf16[576,128]{1,0:T(8,128)(2,1)S(1)} %get-tuple-element.67), channel_id=1, source_target_pairs={{0,3},{1,2},{2,1},{3,0},{4,7},{5,6},{6,5},{7,4},{8,11},{9,10},{10,... | collective-permute-start | bytes 442376 | tf_op jit(solution)/shard_map/ppermute | solution.py:437
  6.5 11.8 %collective-permute-start = (bf16[576,128]{1,0:T(8,128)(2,1)S(1)}, bf16[576,128]{1,0:T(8,128)(2,1)S(1)}, u32[]{:S(2)}, u32[]{:S(2)}) collective-permute-start(bf16[576,128]{1,0:T(8,128)(2,1)S(1)} %get-tuple-element.61), channel_id=1, source_target_pairs={{0,1},{1,0},{2,3},{3,2},{4,5},{5,4},{6,7},{7,6},{8,9},{9,8},{10,11... | collective-permute-start | bytes 442376 | tf_op jit(solution)/shard_map/ppermute | solution.py:437
  6.7 11.6 %collective-permute-start.1 = (bf16[576,128]{1,0:T(8,128)(2,1)S(1)}, bf16[576,128]{1,0:T(8,128)(2,1)S(1)}, u32[]{:S(2)}, u32[]{:S(2)}) collective-permute-start(bf16[576,128]{1,0:T(8,128)(2,1)S(1)} %get-tuple-element.62), channel_id=1, source_target_pairs={{0,2},{1,3},{2,0},{3,1},{4,6},{5,7},{6,4},{7,5},{8,10},{9,11},{10,... | collective-permute-start | bytes 442376 | tf_op jit(solution)/shard_map/ppermute | solution.py:437
  8.6 10.1 %collective-permute-start.2 = (bf16[576,128]{1,0:T(8,128)(2,1)S(1)}, bf16[576,128]{1,0:T(8,128)(2,1)S(1)}, u32[]{:S(2)}, u32[]{:S(2)}) collective-permute-start(bf16[576,128]{1,0:T(8,128)(2,1)S(1)} %get-tuple-element.63), channel_id=1, source_target_pairs={{0,3},{1,2},{2,1},{3,0},{4,7},{5,6},{6,5},{7,4},{8,11},{9,10},{10,... | collective-permute-start | bytes 442376 | tf_op jit(solution)/shard_map/ppermute | solution.py:437
  15.9 9.4 %collective-permute-start.7 = (bf16[576,128]{1,0:T(8,128)(2,1)S(1)}, bf16[576,128]{1,0:T(8,128)(2,1)S(1)}, u32[]{:S(2)}, u32[]{:S(2)}) collective-permute-start(bf16[576,128]{1,0:T(8,128)(2,1)S(1)} %get-tuple-element.73), channel_id=1, source_target_pairs={{0,1},{1,0},{2,3},{3,2},{4,5},{5,4},{6,7},{7,6},{8,9},{9,8},{10,11... | collective-permute-start | bytes 442376 | tf_op jit(solution)/shard_map/ppermute | solution.py:437
  16.3 9.0 %collective-permute-start.8 = (bf16[576,128]{1,0:T(8,128)(2,1)S(1)}, bf16[576,128]{1,0:T(8,128)(2,1)S(1)}, u32[]{:S(2)}, u32[]{:S(2)}) collective-permute-start(bf16[576,128]{1,0:T(8,128)(2,1)S(1)} %get-tuple-element.74), channel_id=1, source_target_pairs={{0,2},{1,3},{2,0},{3,1},{4,6},{5,7},{6,4},{7,5},{8,10},{9,11},{10,... | collective-permute-start | bytes 442376 | tf_op jit(solution)/shard_map/ppermute | solution.py:437
  18.3 7.1 %collective-permute-start.9 = (bf16[576,128]{1,0:T(8,128)(2,1)S(1)}, bf16[576,128]{1,0:T(8,128)(2,1)S(1)}, u32[]{:S(2)}, u32[]{:S(2)}) collective-permute-start(bf16[576,128]{1,0:T(8,128)(2,1)S(1)} %get-tuple-element.75), channel_id=1, source_target_pairs={{0,3},{1,2},{2,1},{3,0},{4,7},{5,6},{6,5},{7,4},{8,11},{9,10},{10,... | collective-permute-start | bytes 442376 | tf_op jit(solution)/shard_map/ppermute | solution.py:437
  20.9 13.4 %copy-start.2 = (bf16[1,8,48,768]{3,2,1,0:T(8,128)(2,1)S(1)}, bf16[1,8,48,768]{3,2,1,0:T(8,128)(2,1)}, u32[]{:S(2)}) copy-start(bf16[1,8,48,768]{3,2,1,0:T(8,128)(2,1)} %grid_ref.6) | copy-start | bytes 1769476
  20.9 4.4 %collective-permute-start.6 = (bf16[288,128]{1,0:T(8,128)(2,1)S(1)}, bf16[288,128]{1,0:T(8,128)(2,1)S(1)}, u32[]{:S(2)}, u32[]{:S(2)}) collective-permute-start(bf16[288,128]{1,0:T(8,128)(2,1)S(1)} %get-tuple-element.85), channel_id=1, source_target_pairs={{0,4},{4,0},{8,12},{12,8},{16,20},{20,16},{24,28},{28,24},{1,5},{5... | collective-permute-start | bytes 221192 | tf_op jit(solution)/shard_map/ppermute | solution.py:437
  22.6 16.5 %copy-start.4 = (bf16[1,8,48,768]{3,2,1,0:T(8,128)(2,1)S(1)}, bf16[1,8,48,768]{3,2,1,0:T(8,128)(2,1)}, u32[]{:S(2)}) copy-start(bf16[1,8,48,768]{3,2,1,0:T(8,128)(2,1)} %grid_ref.7) | copy-start | bytes 1769476
  25.4 4.4 %collective-permute-start.10 = (bf16[288,128]{1,0:T(8,128)(2,1)S(1)}, bf16[288,128]{1,0:T(8,128)(2,1)S(1)}, u32[]{:S(2)}, u32[]{:S(2)}) collective-permute-start(bf16[288,128]{1,0:T(8,128)(2,1)S(1)} %add_convert_fusion.2), channel_id=1, source_target_pairs={{0,8},{4,12},{8,0},{12,4},{16,24},{20,28},{24,16},{28,20},{1,9},{5... | collective-permute-start | bytes 221192 | tf_op jit(solution)/shard_map/ppermute | solution.py:437
  27.2 8.1 %collective-permute-start.12 = (bf16[576,128]{1,0:T(8,128)(2,1)S(1)}, bf16[576,128]{1,0:T(8,128)(2,1)S(1)}, u32[]{:S(2)}, u32[]{:S(2)}) collective-permute-start(bf16[576,128]{1,0:T(8,128)(2,1)S(1)} %get-tuple-element.97), channel_id=1, source_target_pairs={{0,2},{1,3},{2,0},{3,1},{4,6},{5,7},{6,4},{7,5},{8,10},{9,11},{10,... | collective-permute-start | bytes 442376 | tf_op jit(solution)/shard_map/ppermute | solution.py:437
  29.8 5.5 %collective-permute-start.11 = (bf16[288,128]{1,0:T(8,128)(2,1)S(1)}, bf16[288,128]{1,0:T(8,128)(2,1)S(1)}, u32[]{:S(2)}, u32[]{:S(2)}) collective-permute-start(bf16[288,128]{1,0:T(8,128)(2,1)S(1)} %add_convert_fusion.1), channel_id=1, source_target_pairs={{0,16},{4,20},{8,24},{12,28},{16,0},{20,4},{24,8},{28,12},{1,17},{... | collective-permute-start | bytes 221192 | tf_op jit(solution)/shard_map/ppermute | solution.py:437
  32.7 5.8 %collective-permute-start.15 = (bf16[576,128]{1,0:T(8,128)(2,1)S(1)}, bf16[576,128]{1,0:T(8,128)(2,1)S(1)}, u32[]{:S(2)}, u32[]{:S(2)}) collective-permute-start(bf16[576,128]{1,0:T(8,128)(2,1)S(1)} %get-tuple-element.101), channel_id=1, source_target_pairs={{0,1},{1,0},{2,3},{3,2},{4,5},{5,4},{6,7},{7,6},{8,9},{9,8},{10,11... | collective-permute-start | bytes 442376 | tf_op jit(solution)/shard_map/ppermute | solution.py:437
  32.7 6.3 %collective-permute-start.16 = (bf16[576,128]{1,0:T(8,128)(2,1)S(1)}, bf16[576,128]{1,0:T(8,128)(2,1)S(1)}, u32[]{:S(2)}, u32[]{:S(2)}) collective-permute-start(bf16[576,128]{1,0:T(8,128)(2,1)S(1)} %get-tuple-element.103), channel_id=1, source_target_pairs={{0,3},{1,2},{2,1},{3,0},{4,7},{5,6},{6,5},{7,4},{8,11},{9,10},{10,... | collective-permute-start | bytes 442376 | tf_op jit(solution)/shard_map/ppermute | solution.py:437
  35.4 4.7 %collective-permute-start.13 = (bf16[288,128]{1,0:T(8,128)(2,1)S(1)}, bf16[288,128]{1,0:T(8,128)(2,1)S(1)}, u32[]{:S(2)}, u32[]{:S(2)}) collective-permute-start(bf16[288,128]{1,0:T(8,128)(2,1)S(1)} %add_convert_fusion.refs_1_), channel_id=1, source_target_pairs={{0,1},{1,0},{2,3},{3,2},{4,5},{5,4},{6,7},{7,6},{8,9},{9,8},{10,11... | collective-permute-start | bytes 221192 | tf_op jit(solution)/shard_map/ppermute | solution.py:437
  35.5 5.6 %collective-permute-start.14 = (bf16[288,128]{1,0:T(8,128)(2,1)S(1)}, bf16[288,128]{1,0:T(8,128)(2,1)S(1)}, u32[]{:S(2)}, u32[]{:S(2)}) collective-permute-start(bf16[288,128]{1,0:T(8,128)(2,1)S(1)} %add_convert_fusion.refs_1_), channel_id=1, source_target_pairs={{0,6},{1,7},{2,4},{3,5},{4,2},{5,3},{6,0},{7,1},{8,14},{9,15},{10,... | collective-permute-start | bytes 221192 | tf_op jit(solution)/shard_map/ppermute | solution.py:528
  38.0 4.7 %collective-permute-start.17 = (bf16[288,128]{1,0:T(8,128)(2,1)S(1)}, bf16[288,128]{1,0:T(8,128)(2,1)S(1)}, u32[]{:S(2)}, u32[]{:S(2)}) collective-permute-start(bf16[288,128]{1,0:T(8,128)(2,1)S(1)} %add_convert_fusion.refs_1_), channel_id=1, source_target_pairs={{0,2},{1,3},{2,0},{3,1},{4,6},{5,7},{6,4},{7,5},{8,10},{9,11},{10,... | collective-permute-start | bytes 221192 | tf_op jit(solution)/shard_map/ppermute | solution.py:528
  38.5 4.4 %collective-permute-start.19 = (bf16[288,128]{1,0:T(8,128)(2,1)S(1)}, bf16[288,128]{1,0:T(8,128)(2,1)S(1)}, u32[]{:S(2)}, u32[]{:S(2)}) collective-permute-start(bf16[288,128]{1,0:T(8,128)(2,1)S(1)} %add_convert_fusion.refs_1_), channel_id=1, source_target_pairs={{0,4},{1,5},{2,6},{3,7},{4,0},{5,1},{6,2},{7,3},{8,12},{9,13},{10,... | collective-permute-start | bytes 221192 | tf_op jit(solution)/shard_map/ppermute | solution.py:528
  41.1 2.1 %collective-permute-start.21 = (bf16[288,128]{1,0:T(8,128)(2,1)S(1)}, bf16[288,128]{1,0:T(8,128)(2,1)S(1)}, u32[]{:S(2)}, u32[]{:S(2)}) collective-permute-start(bf16[288,128]{1,0:T(8,128)(2,1)S(1)} %collective-permute-done.14.refs_0_), channel_id=1, source_target_pairs={{0,1},{1,0},{2,3},{3,2},{4,5},{5,4},{6,7},{7,6},{8,9},{9,8},{10,11... | collective-permute-start | bytes 221192 | tf_op jit(solution)/shard_map/ppermute | solution.py:437
  42.6 1.5 %collective-permute-start.18 = (bf16[288,128]{1,0:T(8,128)(2,1)S(1)}, bf16[288,128]{1,0:T(8,128)(2,1)S(1)}, u32[]{:S(2)}, u32[]{:S(2)}) collective-permute-start(bf16[288,128]{1,0:T(8,128)(2,1)S(1)} %collective-permute-done.17.refs_0_), channel_id=1, source_target_pairs={{0,1},{1,0},{2,3},{3,2},{4,5},{5,4},{6,7},{7,6},{8,9},{9,8},{10,11... | collective-permute-start | bytes 221192 | tf_op jit(solution)/shard_map/ppermute | solution.py:437
  42.8 1.3 %collective-permute-start.20 = (bf16[288,128]{1,0:T(8,128)(2,1)S(1)}, bf16[288,128]{1,0:T(8,128)(2,1)S(1)}, u32[]{:S(2)}, u32[]{:S(2)}) collective-permute-start(bf16[288,128]{1,0:T(8,128)(2,1)S(1)} %collective-permute-done.19.refs_2_), channel_id=1, source_target_pairs={{0,1},{1,0},{2,3},{3,2},{4,5},{5,4},{6,7},{7,6},{8,9},{9,8},{10,11... | collective-permute-start | bytes 221192 | tf_op jit(solution)/shard_map/ppermute | solution.py:437
  (4 other events, 7.1 us)
